TPU v7x, 32 devices: a whole 2x2x4 slice. The times are simulated.
32 devices in a mesh: dp: 2 (over x), ctx: 16 (over z, y, core).
Axes of the slice: x: 2, y: 2, z: 4, core: 2. Of those that a mesh axis runs over, the one named last changes fastest.
Arguments:
- level_input: bfloat16 [2, 16384, 256], P('dp', 'ctx'), may hold values from -6 to 6
- saved_forward: bfloat16 [3, 2, 16384, 256], P(None, 'dp', 'ctx'), may hold values from -6 to 6
- saved_reverse: bfloat16 [3, 2, 16384, 256], P(None, 'dp', 'ctx'), may hold values from -6 to 6
- filters: float32 [2, 2, 2, 256], replicated, may hold values from -2.5 to 2.5
- mixing: float32 [2, 5, 256], replicated, may hold values from -3 to 3
- cotangent: bfloat16 [2, 16384, 256], P('dp', 'ctx'), may hold values from -33 to 33
Outputs:
- grad_input: bfloat16 [2, 16384, 256], P('dp', 'ctx')
- grad_filters: float32 [2, 2, 2, 256], replicated
- grad_mixing: float32 [2, 5, 256], replicated
All inputs are finite; a program needn't handle non-finite values.
Results may differ from a plain program's by a relative error of at most 0.0065.
Values may be sent and summed in bfloat16 or wider, within the bound.
A program may use at most 64 MiB of HBM per device.

v0:
```python
import math

import jax
import jax.numpy as jnp
from jax import lax
from jax.sharding import PartitionSpec as P

BASE = 128


def from_behind(block, axis, distance):
    devices = range(lax.axis_size(axis))
    route = [(i - distance, i) for i in devices if i - distance in devices]
    return lax.ppermute(block, axis, route)


def totals(values):
    return jnp.sum(values, axis=(0, 1))


def level_terms(gains, weight, s_a, s_y, t_a, t_y):
    filt = jnp.stack([jnp.stack([s_a, t_a]), jnp.stack([weight * s_y, weight * t_y])])
    high = gains[1, 0] * s_y + gains[1, 1] * t_y
    final = gains[0, 0] * s_y + gains[0, 1] * t_y
    return (filt, high, final)


def body(level_input, saved_forward, saved_reverse, filters, mixing, cotangent):
    levels = saved_forward.shape[0] + 1
    span = level_input.shape[1]
    width = level_input.shape[2]
    dy = cotangent.astype(jnp.float32)
    inputs_fwd = [level_input] + [saved_forward[i] for i in range(levels - 1)]
    inputs_rev = [level_input] + [saved_reverse[i] for i in range(levels - 1)]
    gains_fwd = filters[0]
    gains_rev = filters[1]
    grad_fwd = mixing[0, levels] * dy
    grad_rev = mixing[1, levels] * dy
    filt_total = jnp.zeros((2, 2, 2, width), jnp.float32)
    mix_total = jnp.zeros((2, levels + 1, width), jnp.float32)
    for level in reversed(range(levels)):
        dist = BASE * 2**level
        keep = span - dist
        plain_fwd = inputs_fwd[level].astype(jnp.float32)
        plain_rev = inputs_rev[level].astype(jnp.float32)
        weight_fwd = mixing[0, level]
        weight_rev = mixing[1, level]
        rim_fwd = from_behind(inputs_fwd[level][:, keep:], "ctx", 1)
        rim_rev = from_behind(inputs_rev[level][:, :dist], "ctx", -1)
        near_fwd = jnp.concatenate([rim_fwd.astype(jnp.float32), plain_fwd[:, :keep]], axis=1)
        near_rev = jnp.concatenate([plain_rev[:, dist:], rim_rev.astype(jnp.float32)], axis=1)
        cross_fwd = (totals(grad_fwd * near_fwd), totals(dy * near_fwd))
        cross_rev = (totals(grad_rev * near_rev), totals(dy * near_rev))
        tapped_fwd = gains_fwd[0, 0] * grad_fwd + gains_fwd[1, 0] * (weight_fwd * dy)
        tapped_rev = gains_rev[0, 0] * grad_rev + gains_rev[1, 0] * (weight_rev * dy)
        back_fwd = from_behind(tapped_fwd[:, :dist], "ctx", -1)
        back_rev = from_behind(tapped_rev[:, keep:], "ctx", 1)
        moved_fwd = jnp.concatenate([tapped_fwd[:, dist:], back_fwd], axis=1)
        moved_rev = jnp.concatenate([back_rev, tapped_rev[:, :keep]], axis=1)
        last = level == levels - 1
        filt_fwd, high_fwd, final_fwd = level_terms(
            gains_fwd,
            weight_fwd,
            cross_fwd[0],
            cross_fwd[1],
            totals(grad_fwd * plain_fwd),
            totals(dy * plain_fwd),
        )
        filt_rev, high_rev, final_rev = level_terms(
            gains_rev,
            weight_rev,
            cross_rev[0],
            cross_rev[1],
            totals(grad_rev * plain_rev),
            totals(dy * plain_rev),
        )
        filt_part = jnp.stack([filt_fwd, filt_rev])
        mix_part = jnp.zeros((2, levels + 1, width), jnp.float32)
        mix_part = mix_part.at[0, level].set(high_fwd).at[1, level].set(high_rev)
        if last:
            mix_part = mix_part.at[0, levels].set(final_fwd).at[1, levels].set(final_rev)
        filt_sum, mix_sum = lax.psum((filt_part, mix_part), ("dp", "ctx"))
        filt_total = filt_total + filt_sum
        mix_total = mix_total + mix_sum
        grad_fwd = gains_fwd[0, 1] * grad_fwd + gains_fwd[1, 1] * (weight_fwd * dy) + moved_fwd
        grad_rev = gains_rev[0, 1] * grad_rev + gains_rev[1, 1] * (weight_rev * dy) + moved_rev
    count = level_input.shape[0] * lax.axis_size("dp") * span * lax.axis_size("ctx")
    factor = 1.0 / math.sqrt(count)
    grad_input = (grad_fwd + grad_rev).astype(jnp.bfloat16)
    return (grad_input, filt_total * factor, mix_total * factor)


def solution(mesh):
    return jax.shard_map(
        body,
        mesh=mesh,
        in_specs=(
            P("dp", "ctx", None),
            P(None, "dp", "ctx", None),
            P(None, "dp", "ctx", None),
            P(),
            P(),
            P("dp", "ctx", None),
        ),
        out_specs=(P("dp", "ctx", None), P(), P()),
        check_vma=False,
    )
```

profile of v0, /device:TPU:1, one launch (start us, length us, event | category | flops | bytes accessed | tf_op | source)
XLA Modules:
  0.0 188.0 jit_solution(11397014160844264296)
XLA Ops:
  0.6 0.9 fusion.83
  1.6 0.7 fusion.84
  2.4 1.3 fusion.37
  3.6 4.7 %collective-permute-start.4 = (f32[1,1024,256]{2,1,0:T(8,128)S(1)}, f32[1,1024,256]{2,1,0:T(8,128)S(1)}, u32[]{:S(2)}, u32[]{:S(2)}) collective-permute-start(f32[1,1024,256]{2,1,0:T(8,128)S(1)} %fusion.37), channel_id=1, source_target_pairs={{0,1},{1,2},{2,3},{3,4},{4,5},{5,6},{6,7},{7,8},{8,9},{9,10},{10,1... | collective-permute-start | bytes 3145736 | tf_op jit(solution)/shard_map/ppermute | solution.py:14
  8.6 1.9 %collective-permute-start.13 = (bf16[1,256,256]{2,1,0:T(8,128)(2,1)S(1)}, bf16[1,256,256]{2,1,0:T(8,128)(2,1)S(1)}, u32[]{:S(2)}, u32[]{:S(2)}) collective-permute-start(bf16[1,256,256]{2,1,0:T(8,128)(2,1)S(1)} %slice.507), channel_id=1, source_target_pairs={{1,0},{2,1},{3,2},{4,3},{5,4},{6,5},{7,6},{8,7},{9,8},{10,9},{11,1... | collective-permute-start | bytes 393224 | tf_op jit(solution)/shard_map/ppermute | solution.py:14
  10.6 1.9 %collective-permute-start.11 = (bf16[1,512,256]{2,1,0:T(8,128)(2,1)S(1)}, bf16[1,512,256]{2,1,0:T(8,128)(2,1)S(1)}, u32[]{:S(2)}, u32[]{:S(2)}) collective-permute-start(bf16[1,512,256]{2,1,0:T(8,128)(2,1)S(1)} %slice.503), channel_id=1, source_target_pairs={{1,0},{2,1},{3,2},{4,3},{5,4},{6,5},{7,6},{8,7},{9,8},{10,9},{11,1... | collective-permute-start | bytes 786440 | tf_op jit(solution)/shard_map/ppermute | solution.py:14
  12.5 11.7 %collective-permute-done.4 = f32[1,1024,256]{2,1,0:T(8,128)S(1)} collective-permute-done((f32[1,1024,256]{2,1,0:T(8,128)S(1)}, f32[1,1024,256]{2,1,0:T(8,128)S(1)}, u32[]{:S(2)}, u32[]{:S(2)}) %collective-permute-start.4) | collective-permute-done | bytes 1048608 | tf_op jit(solution)/shard_map/ppermute | solution.py:14
  24.7 4.5 %collective-permute-start.5 = (f32[1,512,256]{2,1,0:T(8,128)S(1)}, f32[1,512,256]{2,1,0:T(8,128)S(1)}, u32[]{:S(2)}, u32[]{:S(2)}) collective-permute-start(f32[1,512,256]{2,1,0:T(8,128)S(1)} %get-tuple-element.177), channel_id=1, source_target_pairs={{0,1},{1,2},{2,3},{3,4},{4,5},{5,6},{6,7},{7,8},{8,9},{9,10},{10,1... | collective-permute-start | bytes 1572872 | tf_op jit(solution)/shard_map/ppermute | solution.py:14
  29.5 1.9 %collective-permute-start.12 = (bf16[1,256,256]{2,1,0:T(8,128)(2,1)S(1)}, bf16[1,256,256]{2,1,0:T(8,128)(2,1)S(1)}, u32[]{:S(2)}, u32[]{:S(2)}) collective-permute-start(bf16[1,256,256]{2,1,0:T(8,128)(2,1)S(1)} %slice.504), channel_id=1, source_target_pairs={{0,1},{1,2},{2,3},{3,4},{4,5},{5,6},{6,7},{7,8},{8,9},{9,10},{10,1... | collective-permute-start | bytes 393224 | tf_op jit(solution)/shard_map/ppermute | solution.py:14
  31.5 1.9 %collective-permute-start.8 = (bf16[1,1024,256]{2,1,0:T(8,128)(2,1)S(1)}, bf16[1,1024,256]{2,1,0:T(8,128)(2,1)S(1)}, u32[]{:S(2)}, u32[]{:S(2)}) collective-permute-start(bf16[1,1024,256]{2,1,0:T(8,128)(2,1)S(1)} %get-tuple-element.172), channel_id=1, source_target_pairs={{0,1},{1,2},{2,3},{3,4},{4,5},{5,6},{6,7},{7,8},{8,9},{9,10},{10,1... | collective-permute-start | bytes 1572872 | tf_op jit(solution)/shard_map/ppermute | solution.py:14
  33.7 2.4 %collective-permute-start.9 = (bf16[1,1024,256]{2,1,0:T(8,128)(2,1)S(1)}, bf16[1,1024,256]{2,1,0:T(8,128)(2,1)S(1)}, u32[]{:S(2)}, u32[]{:S(2)}) collective-permute-start(bf16[1,1024,256]{2,1,0:T(8,128)(2,1)S(1)} %get-tuple-element.169), channel_id=1, source_target_pairs={{1,0},{2,1},{3,2},{4,3},{5,4},{6,5},{7,6},{8,7},{9,8},{10,9},{11,1... | collective-permute-start | bytes 1572872 | tf_op jit(solution)/shard_map/ppermute | solution.py:14
  36.2 1.9 %collective-permute-start.15 = (bf16[1,128,256]{2,1,0:T(8,128)(2,1)S(1)}, bf16[1,128,256]{2,1,0:T(8,128)(2,1)S(1)}, u32[]{:S(2)}, u32[]{:S(2)}) collective-permute-start(bf16[1,128,256]{2,1,0:T(8,128)(2,1)S(1)} %get-tuple-element.185), channel_id=1, source_target_pairs={{1,0},{2,1},{3,2},{4,3},{5,4},{6,5},{7,6},{8,7},{9,8},{10,9},{11,1... | collective-permute-start | bytes 196616 | tf_op jit(solution)/shard_map/ppermute | solution.py:14
  38.1 1.2 multiply_reduce_fusion.8
  39.6 3.6 %collective-permute-start.6 = (f32[1,256,256]{2,1,0:T(8,128)S(1)}, f32[1,256,256]{2,1,0:T(8,128)S(1)}, u32[]{:S(2)}, u32[]{:S(2)}) collective-permute-start(f32[1,256,256]{2,1,0:T(8,128)S(1)} %slice.496), channel_id=1, source_target_pairs={{0,1},{1,2},{2,3},{3,4},{4,5},{5,6},{6,7},{7,8},{8,9},{9,10},{10,1... | collective-permute-start | bytes 786440 | tf_op jit(solution)/shard_map/ppermute | solution.py:14
  44.0 0.9 collective-permute-done.15
  44.9 2.0 %collective-permute-start.10 = (bf16[1,512,256]{2,1,0:T(8,128)(2,1)S(1)}, bf16[1,512,256]{2,1,0:T(8,128)(2,1)S(1)}, u32[]{:S(2)}, u32[]{:S(2)}) collective-permute-start(bf16[1,512,256]{2,1,0:T(8,128)(2,1)S(1)} %slice.500), channel_id=1, source_target_pairs={{0,1},{1,2},{2,3},{3,4},{4,5},{5,6},{6,7},{7,8},{8,9},{9,10},{10,1... | collective-permute-start | bytes 786440 | tf_op jit(solution)/shard_map/ppermute | solution.py:14
  46.9 6.1 %collective-permute-start.14 = (bf16[1,128,256]{2,1,0:T(8,128)(2,1)S(1)}, bf16[1,128,256]{2,1,0:T(8,128)(2,1)S(1)}, u32[]{:S(2)}, u32[]{:S(2)}) collective-permute-start(bf16[1,128,256]{2,1,0:T(8,128)(2,1)S(1)} %get-tuple-element.186), channel_id=1, source_target_pairs={{0,1},{1,2},{2,3},{3,4},{4,5},{5,6},{6,7},{7,8},{8,9},{9,10},{10,1... | collective-permute-start | bytes 196616 | tf_op jit(solution)/shard_map/ppermute | solution.py:14
  53.1 1.6 multiply_reduce_fusion.1
  55.1 1.9 %collective-permute-start = (f32[1,1024,256]{2,1,0:T(8,128)S(1)}, f32[1,1024,256]{2,1,0:T(8,128)S(1)}, u32[]{:S(2)}, u32[]{:S(2)}) collective-permute-start(f32[1,1024,256]{2,1,0:T(8,128)S(1)} %get-tuple-element.182), channel_id=1, source_target_pairs={{1,0},{2,1},{3,2},{4,3},{5,4},{6,5},{7,6},{8,7},{9,8},{10,9},{11,1... | collective-permute-start | bytes 3145736 | tf_op jit(solution)/shard_map/ppermute | solution.py:14
  57.6 0.7 fusion.88
  58.3 0.8 and_reduce_fusion
  59.2 0.6 fusion.90
  60.0 0.7 slice.498
  60.6 3.6 %collective-permute-start.7 = (f32[1,128,256]{2,1,0:T(8,128)}, f32[1,128,256]{2,1,0:T(8,128)}, u32[]{:S(2)}, u32[]{:S(2)}) collective-permute-start(f32[1,128,256]{2,1,0:T(8,128)} %slice.498), channel_id=1, source_target_pairs={{0,1},{1,2},{2,3},{3,4},{4,5},{5,6},{6,7},{7,8},{8,9},{9,10},{10,1... | collective-permute-start | bytes 393224 | tf_op jit(solution)/shard_map/ppermute | solution.py:14
  64.9 1.3 bitcast_multiply_fusion.1
  66.2 5.0 %collective-permute-done = f32[1,1024,256]{2,1,0:T(8,128)S(1)} collective-permute-done((f32[1,1024,256]{2,1,0:T(8,128)S(1)}, f32[1,1024,256]{2,1,0:T(8,128)S(1)}, u32[]{:S(2)}, u32[]{:S(2)}) %collective-permute-start) | collective-permute-done | bytes 1048608 | tf_op jit(solution)/shard_map/ppermute | solution.py:14
  71.7 1.9 %collective-permute-start.1 = (f32[1,512,256]{2,1,0:T(8,128)S(1)}, f32[1,512,256]{2,1,0:T(8,128)S(1)}, u32[]{:S(2)}, u32[]{:S(2)}) collective-permute-start(f32[1,512,256]{2,1,0:T(8,128)S(1)} %get-tuple-element.180), channel_id=1, source_target_pairs={{1,0},{2,1},{3,2},{4,3},{5,4},{6,5},{7,6},{8,7},{9,8},{10,9},{11,1... | collective-permute-start | bytes 1572872 | tf_op jit(solution)/shard_map/ppermute | solution.py:14
  75.4 7.1 %collective-permute-done.1 = f32[1,512,256]{2,1,0:T(8,128)S(1)} collective-permute-done((f32[1,512,256]{2,1,0:T(8,128)S(1)}, f32[1,512,256]{2,1,0:T(8,128)S(1)}, u32[]{:S(2)}, u32[]{:S(2)}) %collective-permute-start.1) | collective-permute-done | bytes 524320 | tf_op jit(solution)/shard_map/ppermute | solution.py:14
  82.5 1.2 multiply_reduce_fusion.10
  83.9 1.9 %collective-permute-start.2 = (f32[1,256,256]{2,1,0:T(8,128)S(1)}, f32[1,256,256]{2,1,0:T(8,128)S(1)}, u32[]{:S(2)}, u32[]{:S(2)}) collective-permute-start(f32[1,256,256]{2,1,0:T(8,128)S(1)} %slice.487), channel_id=1, source_target_pairs={{1,0},{2,1},{3,2},{4,3},{5,4},{6,5},{7,6},{8,7},{9,8},{10,9},{11,1... | collective-permute-start | bytes 786440 | tf_op jit(solution)/shard_map/ppermute | solution.py:14
  87.7 4.4 %collective-permute-done.2 = f32[1,256,256]{2,1,0:T(8,128)S(1)} collective-permute-done((f32[1,256,256]{2,1,0:T(8,128)S(1)}, f32[1,256,256]{2,1,0:T(8,128)S(1)}, u32[]{:S(2)}, u32[]{:S(2)}) %collective-permute-start.2) | collective-permute-done | bytes 262176 | tf_op jit(solution)/shard_map/ppermute | solution.py:14
  92.0 1.1 multiply_reduce_fusion.3
  93.4 1.0 slice.488
  94.3 0.7 slice.489
  95.1 1.9 %broadcast_select_fusion = (f32[1,1,256]{2,0,1:T(1,128)}, f32[1,1,256]{2,0,1:T(1,128)}, f32[1,1,256]{2,0,1:T(1,128)}, f32[1,1,256]{2,0,1:T(1,128)}) fusion(pred[]{:T(512)} %get-tuple-element.158, f32[1,1,256]{2,0,1:T(1,128)S(1)} %bitcast.273, f32[1,1,256]{2,0,1:T(1,128)S(1)} %bitcast.275, f32[2,2,256]{2,0,1:T(2,128)S(1)} %get-tuple-element.245, ...), kind=kLoop, calls=%fused_computation.150 | loop fusion | flops 3584 | bytes 14338 | tf_op jit(solution)/shard_map/select.23
  97.0 1.9 scatter.34
  98.8 1.3 multiply_add_fusion.4
  100.2 0.7 scatter.35
  100.9 2.6 %broadcast_select_fusion.1 = f32[1,1,256]{2,0,1:T(1,128)S(1)} fusion(pred[]{:T(512)} %get-tuple-element.159, f32[2,5,256]{2,0,1:T(2,128)S(1)} %scatter.35, s32[]{:T(128)} %bitcast.95, s32[]{:T(128)} %bitcast.96, f32[1,1,256]{2,0,1:T(1,128)} %bitcast.242, f32[1,1,256]{2,0,1:T(1,128)} %bitcast.239, f32[2,2,256]{2,0,1:T(2,128)} %copy-done.4), kind=kLoop, calls=%fused_computation.152 | loop fusion | flops 1024 | bytes 6153 | tf_op jit(solution)/shard_map/select.12
  103.5 1.4 scatter.36
  105.5 2.6 %scatter.44 = f32[2,5,256]{2,0,1:T(2,128)} dynamic-update-slice(f32[2,5,256]{2,0,1:T(2,128)} %broadcast.185.clone, f32[1,1,256]{2,0,1:T(1,128)} %get-tuple-element.226, s32[]{:T(128)} %bitcast.105, s32[]{:T(128)} %bitcast.106, s32[]{:T(128)} %constant.283.clone.1) | dynamic-update-slice | bytes 2052 | tf_op jit(solution)/shard_map/scatter | solution.py:79
  108.1 1.3 scatter.45
  109.4 1.3 scatter.46
  110.7 1.3 scatter.49
  111.9 0.7 maximum_bitcast_fusion.20
  112.6 0.8 bitcast_multiply_fusion.3
  113.5 0.7 maximum_bitcast_fusion.23
  114.1 1.3 maximum_bitcast_fusion.7
  115.4 1.3 maximum_bitcast_fusion.4
  116.7 1.3 maximum_bitcast_fusion.2
  118.0 1.3 maximum_bitcast_fusion
  119.2 0.7 maximum_bitcast_fusion.11
  119.9 1.3 maximum_bitcast_fusion.1
  121.8 2.4 %scatter.40 = f32[2,5,256]{2,0,1:T(2,128)} dynamic-update-slice(f32[2,5,256]{2,0,1:T(2,128)} %broadcast.185.clone.2, f32[1,1,256]{2,0,1:T(1,128)} %get-tuple-element.224, s32[]{:T(128)} %bitcast.99, s32[]{:T(128)} %bitcast.100, s32[]{:T(128)} %constant.283.clone.1) | dynamic-update-slice | bytes 2052 | tf_op jit(solution)/shard_map/scatter | solution.py:79
  124.2 1.3 scatter.41
  125.4 0.7 scatter.39
  126.1 1.3 add_add_fusion
  127.4 0.7 fusion.70
  128.2 47.9 %all-reduce.1 = (f32[2,2,2,256]{3,2,1,0:T(2,128)S(1)}, f32[2,5,256]{2,0,1:T(2,128)}) all-reduce(f32[2,2,2,256]{3,2,1,0:T(2,128)S(1)} %fusion.70, f32[2,5,256]{2,0,1:T(2,128)} %add_add_fusion), channel_id=1, replica_groups=mesh['dp'=2,'ctx'=16] {'dp','ctx'}, use_global_device_ids=true, to_apply=%region_8.0 | all-reduce | flops 4608 | bytes 36864 | tf_op jit(solution)/shard_map/psum | solution.py:82
  176.1 1.3 broadcast_multiply_fusion
  177.4 3.0 %collective-permute-start.3 = (f32[1,128,256]{2,1,0:T(8,128)}, f32[1,128,256]{2,1,0:T(8,128)S(1)}, u32[]{:S(2)}, u32[]{:S(2)}) collective-permute-start(f32[1,128,256]{2,1,0:T(8,128)} %slice.489), channel_id=1, source_target_pairs={{1,0},{2,1},{3,2},{4,3},{5,4},{6,5},{7,6},{8,7},{9,8},{10,9},{11,1... | collective-permute-start | bytes 393224 | tf_op jit(solution)/shard_map/ppermute | solution.py:14
  180.4 0.6 broadcast_multiply_fusion.1
  181.0 4.5 %collective-permute-done.3 = f32[1,128,256]{2,1,0:T(8,128)S(1)} collective-permute-done((f32[1,128,256]{2,1,0:T(8,128)}, f32[1,128,256]{2,1,0:T(8,128)S(1)}, u32[]{:S(2)}, u32[]{:S(2)}) %collective-permute-start.3) | collective-permute-done | bytes 131104 | tf_op jit(solution)/shard_map/ppermute | solution.py:14
  185.5 2.5 %fusion.27 = bf16[1,1024,256]{2,1,0:T(8,128)(2,1)} fusion(bf16[1,1024,256]{2,1,0:T(8,128)(2,1)S(1)} %copy-done, f32[1,128,256]{2,1,0:T(8,128)S(1)} %collective-permute-done.3, f32[1,896,256]{2,1,0:T(8,128)} %slice.488, f32[1,896,256]{2,1,0:T(8,128)S(1)} %slice.499, f32[1,128,256]{2,1,0:T(8,128)} %collective-permute-done.7, ...), kind=kLoop, calls=%fused_computation.52 | loop fusion | flops 3932160 | bytes 5249024 | tf_op jit(solution)/shard_map/convert_element_type | solution.py:89
  (120 shorter events, 9.8 us)
Async XLA Ops:
  0.6 7.7 %copy-start.2 = (bf16[3,1,1024,256]{3,2,1,0:T(8,128)(2,1)S(1)}, bf16[3,1,1024,256]{3,2,1,0:T(8,128)(2,1)}, u32[]{:S(2)}) copy-start(bf16[3,1,1024,256]{3,2,1,0:T(8,128)(2,1)} %param.28) | copy-start | bytes 4718596
  1.6 53.2 %copy-start.23 = (f32[1,1,256]{2,0,1:T(1,128)}, f32[1,1,256]{2,0,1:T(1,128)S(1)}, u32[]{:S(2)}) copy-start(f32[1,1,256]{2,0,1:T(1,128)S(1)} %get-tuple-element.205) | copy-start | bytes 3076
  1.6 91.6 %copy-start.24 = (f32[1,1,256]{2,0,1:T(1,128)}, f32[1,1,256]{2,0,1:T(1,128)S(1)}, u32[]{:S(2)}) copy-start(f32[1,1,256]{2,0,1:T(1,128)S(1)} %get-tuple-element.209) | copy-start | bytes 3076
  2.3 92.7 %copy-start.4 = (f32[2,2,256]{2,0,1:T(2,128)}, f32[2,2,256]{2,0,1:T(2,128)S(1)}, u32[]{:S(2)}) copy-start(f32[2,2,256]{2,0,1:T(2,128)S(1)} %get-tuple-element.245) | copy-start | bytes 12292
  2.3 50.8 %copy-start.5 = (f32[1,1,256]{2,0,1:T(1,128)}, f32[1,1,256]{2,0,1:T(1,128)S(1)}, u32[]{:S(2)}) copy-start(f32[1,1,256]{2,0,1:T(1,128)S(1)} %get-tuple-element.228) | copy-start | bytes 3076
  2.3 50.8 %copy-start.6 = (f32[1,1,256]{2,0,1:T(1,128)}, f32[1,1,256]{2,0,1:T(1,128)S(1)}, u32[]{:S(2)}) copy-start(f32[1,1,256]{2,0,1:T(1,128)S(1)} %get-tuple-element.231) | copy-start | bytes 3076
  3.6 20.6 %copy-start = (bf16[1,1024,256]{2,1,0:T(8,128)(2,1)S(1)}, bf16[1,1024,256]{2,1,0:T(8,128)(2,1)}, u32[]{:S(2)}) copy-start(bf16[1,1024,256]{2,1,0:T(8,128)(2,1)} %param.31) | copy-start | bytes 1572868
  3.6 20.6 %collective-permute-start.4 = (f32[1,1024,256]{2,1,0:T(8,128)S(1)}, f32[1,1024,256]{2,1,0:T(8,128)S(1)}, u32[]{:S(2)}, u32[]{:S(2)}) collective-permute-start(f32[1,1024,256]{2,1,0:T(8,128)S(1)} %fusion.37), channel_id=1, source_target_pairs={{0,1},{1,2},{2,3},{3,4},{4,5},{5,6},{6,7},{7,8},{8,9},{9,10},{10,1... | collective-permute-start | bytes 3145736 | tf_op jit(solution)/shard_map/ppermute | solution.py:14
  8.6 25.1 %collective-permute-start.13 = (bf16[1,256,256]{2,1,0:T(8,128)(2,1)S(1)}, bf16[1,256,256]{2,1,0:T(8,128)(2,1)S(1)}, u32[]{:S(2)}, u32[]{:S(2)}) collective-permute-start(bf16[1,256,256]{2,1,0:T(8,128)(2,1)S(1)} %slice.507), channel_id=1, source_target_pairs={{1,0},{2,1},{3,2},{4,3},{5,4},{6,5},{7,6},{8,7},{9,8},{10,9},{11,1... | collective-permute-start | bytes 393224 | tf_op jit(solution)/shard_map/ppermute | solution.py:14
  10.6 25.6 %collective-permute-start.11 = (bf16[1,512,256]{2,1,0:T(8,128)(2,1)S(1)}, bf16[1,512,256]{2,1,0:T(8,128)(2,1)S(1)}, u32[]{:S(2)}, u32[]{:S(2)}) collective-permute-start(bf16[1,512,256]{2,1,0:T(8,128)(2,1)S(1)} %slice.503), channel_id=1, source_target_pairs={{1,0},{2,1},{3,2},{4,3},{5,4},{6,5},{7,6},{8,7},{9,8},{10,9},{11,1... | collective-permute-start | bytes 786440 | tf_op jit(solution)/shard_map/ppermute | solution.py:14
  24.6 4.6 %copy-start.3 = (bf16[3,1,1024,256]{3,2,1,0:T(8,128)(2,1)S(1)}, bf16[3,1,1024,256]{3,2,1,0:T(8,128)(2,1)}, u32[]{:S(2)}) copy-start(bf16[3,1,1024,256]{3,2,1,0:T(8,128)(2,1)} %param.27) | copy-start | bytes 4718596
  24.7 8.7 %copy-start.1 = (bf16[1,1024,256]{2,1,0:T(8,128)(2,1)S(1)}, bf16[1,1024,256]{2,1,0:T(8,128)(2,1)}, u32[]{:S(2)}) copy-start(bf16[1,1024,256]{2,1,0:T(8,128)(2,1)} %param.26) | copy-start | bytes 1572868
  24.7 13.4 %collective-permute-start.5 = (f32[1,512,256]{2,1,0:T(8,128)S(1)}, f32[1,512,256]{2,1,0:T(8,128)S(1)}, u32[]{:S(2)}, u32[]{:S(2)}) collective-permute-start(f32[1,512,256]{2,1,0:T(8,128)S(1)} %get-tuple-element.177), channel_id=1, source_target_pairs={{0,1},{1,2},{2,3},{3,4},{4,5},{5,6},{6,7},{7,8},{8,9},{9,10},{10,1... | collective-permute-start | bytes 1572872 | tf_op jit(solution)/shard_map/ppermute | solution.py:14
  29.5 17.3 %collective-permute-start.12 = (bf16[1,256,256]{2,1,0:T(8,128)(2,1)S(1)}, bf16[1,256,256]{2,1,0:T(8,128)(2,1)S(1)}, u32[]{:S(2)}, u32[]{:S(2)}) collective-permute-start(bf16[1,256,256]{2,1,0:T(8,128)(2,1)S(1)} %slice.504), channel_id=1, source_target_pairs={{0,1},{1,2},{2,3},{3,4},{4,5},{5,6},{6,7},{7,8},{8,9},{9,10},{10,1... | collective-permute-start | bytes 393224 | tf_op jit(solution)/shard_map/ppermute | solution.py:14
  31.5 21.6 %collective-permute-start.8 = (bf16[1,1024,256]{2,1,0:T(8,128)(2,1)S(1)}, bf16[1,1024,256]{2,1,0:T(8,128)(2,1)S(1)}, u32[]{:S(2)}, u32[]{:S(2)}) collective-permute-start(bf16[1,1024,256]{2,1,0:T(8,128)(2,1)S(1)} %get-tuple-element.172), channel_id=1, source_target_pairs={{0,1},{1,2},{2,3},{3,4},{4,5},{5,6},{6,7},{7,8},{8,9},{9,10},{10,1... | collective-permute-start | bytes 1572872 | tf_op jit(solution)/shard_map/ppermute | solution.py:14
  33.7 19.4 %collective-permute-start.9 = (bf16[1,1024,256]{2,1,0:T(8,128)(2,1)S(1)}, bf16[1,1024,256]{2,1,0:T(8,128)(2,1)S(1)}, u32[]{:S(2)}, u32[]{:S(2)}) collective-permute-start(bf16[1,1024,256]{2,1,0:T(8,128)(2,1)S(1)} %get-tuple-element.169), channel_id=1, source_target_pairs={{1,0},{2,1},{3,2},{4,3},{5,4},{6,5},{7,6},{8,7},{9,8},{10,9},{11,1... | collective-permute-start | bytes 1572872 | tf_op jit(solution)/shard_map/ppermute | solution.py:14
  36.2 8.7 %collective-permute-start.15 = (bf16[1,128,256]{2,1,0:T(8,128)(2,1)S(1)}, bf16[1,128,256]{2,1,0:T(8,128)(2,1)S(1)}, u32[]{:S(2)}, u32[]{:S(2)}) collective-permute-start(bf16[1,128,256]{2,1,0:T(8,128)(2,1)S(1)} %get-tuple-element.185), channel_id=1, source_target_pairs={{1,0},{2,1},{3,2},{4,3},{5,4},{6,5},{7,6},{8,7},{9,8},{10,9},{11,1... | collective-permute-start | bytes 196616 | tf_op jit(solution)/shard_map/ppermute | solution.py:14
  39.3 25.6 %copy-start.12 = (f32[256]{0:T(256)}, f32[256]{0:T(256)S(1)}, u32[]{:S(2)}) copy-start(f32[256]{0:T(256)S(1)} %get-tuple-element.128) | copy-start | bytes 3076
  39.3 25.6 %copy-start.13 = (f32[256]{0:T(256)}, f32[256]{0:T(256)S(1)}, u32[]{:S(2)}) copy-start(f32[256]{0:T(256)S(1)} %get-tuple-element.131) | copy-start | bytes 3076
  39.3 25.5 %copy-start.14 = (f32[256]{0:T(256)}, f32[256]{0:T(256)S(1)}, u32[]{:S(2)}) copy-start(f32[256]{0:T(256)S(1)} %get-tuple-element.132) | copy-start | bytes 3076
  39.3 25.5 %copy-start.15 = (f32[256]{0:T(256)}, f32[256]{0:T(256)S(1)}, u32[]{:S(2)}) copy-start(f32[256]{0:T(256)S(1)} %get-tuple-element.136) | copy-start | bytes 3076
  39.6 13.5 %collective-permute-start.6 = (f32[1,256,256]{2,1,0:T(8,128)S(1)}, f32[1,256,256]{2,1,0:T(8,128)S(1)}, u32[]{:S(2)}, u32[]{:S(2)}) collective-permute-start(f32[1,256,256]{2,1,0:T(8,128)S(1)} %slice.496), channel_id=1, source_target_pairs={{0,1},{1,2},{2,3},{3,4},{4,5},{5,6},{6,7},{7,8},{8,9},{9,10},{10,1... | collective-permute-start | bytes 786440 | tf_op jit(solution)/shard_map/ppermute | solution.py:14
  43.2 48.8 %copy-start.7 = (f32[1,1,256]{2,0,1:T(1,128)}, f32[1,1,256]{2,0,1:T(1,128)S(1)}, u32[]{:S(2)}) copy-start(f32[1,1,256]{2,0,1:T(1,128)S(1)} %get-tuple-element.232) | copy-start | bytes 3076
  43.3 48.8 %copy-start.8 = (f32[1,1,256]{2,0,1:T(1,128)}, f32[1,1,256]{2,0,1:T(1,128)S(1)}, u32[]{:S(2)}) copy-start(f32[1,1,256]{2,0,1:T(1,128)S(1)} %get-tuple-element.235) | copy-start | bytes 3076
  44.9 15.0 %collective-permute-start.10 = (bf16[1,512,256]{2,1,0:T(8,128)(2,1)S(1)}, bf16[1,512,256]{2,1,0:T(8,128)(2,1)S(1)}, u32[]{:S(2)}, u32[]{:S(2)}) collective-permute-start(bf16[1,512,256]{2,1,0:T(8,128)(2,1)S(1)} %slice.500), channel_id=1, source_target_pairs={{0,1},{1,2},{2,3},{3,4},{4,5},{5,6},{6,7},{7,8},{8,9},{9,10},{10,1... | collective-permute-start | bytes 786440 | tf_op jit(solution)/shard_map/ppermute | solution.py:14
  46.9 12.9 %collective-permute-start.14 = (bf16[1,128,256]{2,1,0:T(8,128)(2,1)S(1)}, bf16[1,128,256]{2,1,0:T(8,128)(2,1)S(1)}, u32[]{:S(2)}, u32[]{:S(2)}) collective-permute-start(bf16[1,128,256]{2,1,0:T(8,128)(2,1)S(1)} %get-tuple-element.186), channel_id=1, source_target_pairs={{0,1},{1,2},{2,3},{3,4},{4,5},{5,6},{6,7},{7,8},{8,9},{9,10},{10,1... | collective-permute-start | bytes 196616 | tf_op jit(solution)/shard_map/ppermute | solution.py:14
  54.7 10.2 %copy-start.16 = (f32[256]{0:T(256)}, f32[256]{0:T(256)S(1)}, u32[]{:S(2)}) copy-start(f32[256]{0:T(256)S(1)} %get-tuple-element.146) | copy-start | bytes 3076
  54.7 10.2 %copy-start.17 = (f32[256]{0:T(256)}, f32[256]{0:T(256)S(1)}, u32[]{:S(2)}) copy-start(f32[256]{0:T(256)S(1)} %get-tuple-element.157) | copy-start | bytes 3076
  54.7 40.3 %copy-start.9 = (f32[256]{0:T(256)}, f32[256]{0:T(256)S(1)}, u32[]{:S(2)}) copy-start(f32[256]{0:T(256)S(1)} %get-tuple-element.154) | copy-start | bytes 3076
  54.7 40.3 %copy-start.18 = (f32[256]{0:T(256)}, f32[256]{0:T(256)S(1)}, u32[]{:S(2)}) copy-start(f32[256]{0:T(256)S(1)} %get-tuple-element.156) | copy-start | bytes 3076
  54.8 3.6 %copy-start.25 = (s32[3]{0:T(128)S(1)}, s32[3]{0:T(128)}, u32[]{:S(2)}) copy-start(s32[3]{0:T(128)} %constant.286.clone.1) | copy-start | bytes 40
  55.1 16.1 %collective-permute-start = (f32[1,1024,256]{2,1,0:T(8,128)S(1)}, f32[1,1024,256]{2,1,0:T(8,128)S(1)}, u32[]{:S(2)}, u32[]{:S(2)}) collective-permute-start(f32[1,1024,256]{2,1,0:T(8,128)S(1)} %get-tuple-element.182), channel_id=1, source_target_pairs={{1,0},{2,1},{3,2},{4,3},{5,4},{6,5},{7,6},{8,7},{9,8},{10,9},{11,1... | collective-permute-start | bytes 3145736 | tf_op jit(solution)/shard_map/ppermute | solution.py:14
  60.6 120.3 %collective-permute-start.7 = (f32[1,128,256]{2,1,0:T(8,128)}, f32[1,128,256]{2,1,0:T(8,128)}, u32[]{:S(2)}, u32[]{:S(2)}) collective-permute-start(f32[1,128,256]{2,1,0:T(8,128)} %slice.498), channel_id=1, source_target_pairs={{0,1},{1,2},{2,3},{3,4},{4,5},{5,6},{6,7},{7,8},{8,9},{9,10},{10,1... | collective-permute-start | bytes 393224 | tf_op jit(solution)/shard_map/ppermute | solution.py:14
  71.7 10.8 %collective-permute-start.1 = (f32[1,512,256]{2,1,0:T(8,128)S(1)}, f32[1,512,256]{2,1,0:T(8,128)S(1)}, u32[]{:S(2)}, u32[]{:S(2)}) collective-permute-start(f32[1,512,256]{2,1,0:T(8,128)S(1)} %get-tuple-element.180), channel_id=1, source_target_pairs={{1,0},{2,1},{3,2},{4,3},{5,4},{6,5},{7,6},{8,7},{9,8},{10,9},{11,1... | collective-permute-start | bytes 1572872 | tf_op jit(solution)/shard_map/ppermute | solution.py:14
  83.6 11.4 %copy-start.10 = (f32[256]{0:T(256)}, f32[256]{0:T(256)S(1)}, u32[]{:S(2)}) copy-start(f32[256]{0:T(256)S(1)} %get-tuple-element.130) | copy-start | bytes 3076
  83.6 11.4 %copy-start.19 = (f32[256]{0:T(256)}, f32[256]{0:T(256)S(1)}, u32[]{:S(2)}) copy-start(f32[256]{0:T(256)S(1)} %get-tuple-element.127) | copy-start | bytes 3076
  83.7 11.4 %copy-start.20 = (f32[256]{0:T(256)}, f32[256]{0:T(256)S(1)}, u32[]{:S(2)}) copy-start(f32[256]{0:T(256)S(1)} %get-tuple-element.129) | copy-start | bytes 3076
  83.7 11.4 %copy-start.21 = (f32[256]{0:T(256)}, f32[256]{0:T(256)S(1)}, u32[]{:S(2)}) copy-start(f32[256]{0:T(256)S(1)} %get-tuple-element.135) | copy-start | bytes 3076
  83.9 8.1 %collective-permute-start.2 = (f32[1,256,256]{2,1,0:T(8,128)S(1)}, f32[1,256,256]{2,1,0:T(8,128)S(1)}, u32[]{:S(2)}, u32[]{:S(2)}) collective-permute-start(f32[1,256,256]{2,1,0:T(8,128)S(1)} %slice.487), channel_id=1, source_target_pairs={{1,0},{2,1},{3,2},{4,3},{5,4},{6,5},{7,6},{8,7},{9,8},{10,9},{11,1... | collective-permute-start | bytes 786440 | tf_op jit(solution)/shard_map/ppermute | solution.py:14
  93.2 1.9 %copy-start.11 = (f32[256]{0:T(256)}, f32[256]{0:T(256)S(1)}, u32[]{:S(2)}) copy-start(f32[256]{0:T(256)S(1)} %get-tuple-element.144) | copy-start | bytes 3076
  93.2 1.9 %copy-start.22 = (f32[256]{0:T(256)}, f32[256]{0:T(256)S(1)}, u32[]{:S(2)}) copy-start(f32[256]{0:T(256)S(1)} %get-tuple-element.142) | copy-start | bytes 3076
  177.4 8.1 %collective-permute-start.3 = (f32[1,128,256]{2,1,0:T(8,128)}, f32[1,128,256]{2,1,0:T(8,128)S(1)}, u32[]{:S(2)}, u32[]{:S(2)}) collective-permute-start(f32[1,128,256]{2,1,0:T(8,128)} %slice.489), channel_id=1, source_target_pairs={{1,0},{2,1},{3,2},{4,3},{5,4},{6,5},{7,6},{8,7},{9,8},{10,9},{11,1... | collective-permute-start | bytes 393224 | tf_op jit(solution)/shard_map/ppermute | solution.py:14
where the time goes:
time: 190 us; the launch traced here: 188 us
  blocking collectives  47.9 us (25%)
  starting transfers between devices  45.3 us (24%)
  other arithmetic  36.5 us (19%)
  waiting for transfers between devices  33.7 us (18%)
  local copies, waits for them, and re-layouts  23.2 us (12%)
    psum x1, blocking collectives, body(): filt_sum, mix_sum = lax.psum((filt_part, mix_part), ('dp', 'ctx'))  47.9 us
    ppermute x16, starting transfers between devices, from_behind(): return lax.ppermute(block, axis, route)  45.3 us
    ppermute x16, waiting for transfers between devices, from_behind(): return lax.ppermute(block, axis, route)  33.7 us
    scatter x8, local copies, waits for them, and re-layouts, body(): mix_part = mix_part.at[0, level].set(high_fwd).at[1, level].set(high_rev)  12.7 us
    another operation x8, other arithmetic, body(): filt_part = jnp.stack([filt_fwd, filt_rev])  7.51 us
    another operation x5, other arithmetic  5.37 us
    reduce_sum x4, other arithmetic, totals(): return jnp.sum(values, axis=(0, 1))  5.08 us
    another operation x16, other arithmetic, level_terms(): jnp.stack([jnp.stack([s_a, t_a]), jnp.stack([weight * s_y, weight * t_y])])  5.05 us
  transfers between devices with their start and end apart: 16, of which 6 were waited for; matrix products, arithmetic and copies ran while one was open for 29% of the time, Pallas kernels for 0%

commit v1 on v0

v1 whole, which is shorter than its diff:
```python
import functools
import math

import jax
import jax.numpy as jnp
from jax import lax
from jax.experimental import pallas as pl
from jax.experimental.pallas import tpu as pltpu
from jax.sharding import PartitionSpec as P

BASE = 128
STRIP = 16
LANES = 128
GROUP = 4
MESH = pl.DeviceIdType.MESH
F32 = jnp.float32


def kernel(
    dims,
    cot,
    first,
    fwd,
    rev,
    filt,
    mix,
    out,
    out_filt,
    out_mix,
    dy,
    inputs,
    result,
    sums,
    coef,
    buf_a,
    buf_b,
    load_sem,
    store_sem,
    send_sem,
    recv_sem,
    send_a,
    recv_a,
    send_b,
    recv_b,
):
    n_dp, n_ctx, units, levels, rows, factor = dims
    chunks = BASE // rows
    groups = n_ctx // GROUP
    width = dy.shape[-1]
    top = levels - 1

    dp = lax.axis_index("dp")
    me = lax.axis_index("ctx")
    q = lax.div(me, GROUP)
    r = lax.rem(me, GROUP)
    half = lax.div(r, 2)
    core = lax.rem(r, 2)
    outer = half == core
    sibling = me + 1 - 2 * core
    partner = me + 2 - 4 * half
    has_next = q < groups - 1
    has_prev = q > 0
    lower = half == 0
    z_sends = jnp.logical_or(jnp.logical_and(lower, has_next), jnp.logical_and(half == 1, has_prev))
    z_recvs = jnp.logical_or(jnp.logical_and(lower, has_prev), jnp.logical_and(half == 1, has_next))

    own_load = pltpu.make_async_copy(cot, dy.at[2], load_sem.at[0])
    in_loads = [
        pltpu.make_async_copy(first, inputs.at[0], load_sem.at[1]),
        pltpu.make_async_copy(fwd, inputs.at[pl.ds(1, top)], load_sem.at[2]),
        pltpu.make_async_copy(rev, inputs.at[pl.ds(levels, top)], load_sem.at[3]),
    ]
    own_load.start()
    for load in in_loads:
        load.start()

    barrier = pltpu.get_barrier_semaphore()
    team = [(a, b) for a in range(n_dp) for b in range(GROUP) if (a, b) != (0, 0)]

    def team_member(a, b):
        return lax.rem(dp + a, n_dp), lax.rem(r + b, GROUP)

    for a, b in team:
        to_dp, to_r = team_member(a, b)
        pl.semaphore_signal(barrier, inc=1, device_id=(to_dp, q * GROUP + to_r), device_id_type=MESH)
    for k in range(1, groups):
        to_q = lax.rem(q + k, groups)
        pl.semaphore_signal(barrier, inc=1, device_id=(dp, to_q * GROUP + r), device_id_type=MESH)
    pl.semaphore_wait(barrier, len(team) + groups - 1)

    def part(ref, c):
        return ref.at[:, pl.ds(pl.multiple_of(c * rows, rows), rows), :]

    def hop(kind, c):
        if kind == 0:
            src, slot, to = part(cot, c), 4 * half, partner
        elif kind == 1:
            src, slot, to = part(cot, c), 1 + 2 * core, sibling
        elif kind == 2:
            src, slot, to = part(dy.at[4 - 4 * half], c), 4 * half, me + 4 - 8 * half
        else:
            src, slot, to = part(dy.at[4 - 4 * core], c), 3 - 2 * core, sibling
        return pltpu.make_async_remote_copy(
            src_ref=src,
            dst_ref=part(dy.at[slot], c),
            send_sem=send_sem.at[kind, c],
            recv_sem=recv_sem.at[kind, c],
            device_id=(dp, to),
            device_id_type=MESH,
        )

    @pl.loop(0, chunks)
    def _(c):
        hop(0, c).start()
        hop(1, c).start()

    @pl.when(jnp.logical_not(z_recvs))
    def _():
        dy[4 * half] = jnp.zeros(dy.shape[1:], dy.dtype)

    @pl.when(jnp.logical_and(jnp.logical_not(z_recvs), outer))
    def _():
        dy[1 + 2 * core] = jnp.zeros(dy.shape[1:], dy.dtype)

    per = 4 + 2 * top
    for b in range(2):
        f00, f01 = filt[b, 0, 0:1, :], filt[b, 0, 1:2, :]
        f10, f11 = filt[b, 1, 0:1, :], filt[b, 1, 1:2, :]
        last, w = mix[b, levels : levels + 1, :], mix[b, top : top + 1, :]
        values = [f01, f00, f01 * last + f11 * w, f00 * last + f10 * w]
        for level in range(top):
            w = mix[b, level : level + 1, :]
            values += [f11 * w, f10 * w]
        for k, value in enumerate(values):
            coef[b * per + k : b * per + k + 1, :] = value
    sums[...] = jnp.zeros(sums.shape, F32)

    n_sums = 2 + 4 * top

    def strip(row, lane):
        rows_at = pl.ds(pl.multiple_of(row, STRIP), STRIP)
        lanes_at = pl.ds(pl.multiple_of(lane, LANES), LANES)
        final = [None] * units
        for b in range(2):

            def place(m):
                return m % units if b == 0 else units - 1 - m % units

            def dy_at(m):
                block = 2 + m // units if b == 0 else 2 - m // units
                return dy[block, place(m), rows_at, lanes_at].astype(F32)

            def input_at(level, m):
                slot = 0 if level == 0 else (level if b == 0 else level + top)
                return inputs[slot, place(m), rows_at, lanes_at].astype(F32)

            def factor_at(k):
                return coef[b * per + k : b * per + k + 1, lanes_at]

            def add(k, value):
                sums[b * n_sums + k, :, lanes_at] += value

            shift = 2**top
            y = [dy_at(m) for m in range(units + 2 * shift - 1)]
            s_y = t_y = None
            for m in range(units):
                p = input_at(top, m)
                s, t = y[m + shift] * p, y[m] * p
                s_y = s if s_y is None else s_y + s
                t_y = t if t_y is None else t_y + t
            add(0, s_y)
            add(1, t_y)
            here, there = factor_at(2), factor_at(3)
            g = [here * y[m] + there * y[m + shift] for m in range(units + shift - 1)]
            for level in reversed(range(top)):
                shift = 2**level
                y = [dy_at(m) for m in range(units + 2 * shift - 1)]
                acc = None
                for m in range(units):
                    p = input_at(level, m)
                    terms = [g[m + shift] * p, y[m + shift] * p, g[m] * p, y[m] * p]
                    acc = terms if acc is None else [u + v for u, v in zip(acc, terms)]
                for k in range(4):
                    add(2 + 4 * level + k, acc[k])
                f01, f00 = factor_at(0), factor_at(1)
                w1, w0 = factor_at(4 + 2 * level), factor_at(5 + 2 * level)
                g = [
                    f01 * g[m] + w1 * y[m] + (f00 * g[m + shift] + w0 * y[m + shift])
                    for m in range(units + shift - 1)
                ]
            for m in range(units):
                final[place(m)] = g[m] if b == 0 else final[place(m)] + g[m]
        for j in range(units):
            result[j, rows_at, lanes_at] = final[j].astype(result.dtype)

    def store(c):
        return pltpu.make_async_copy(part(result, c), part(out, c), store_sem.at[c])

    own_load.wait()
    for load in in_loads:
        load.wait()

    lane_blocks = width // LANES
    pieces = (rows // STRIP) * lane_blocks

    @pl.loop(0, chunks + 2)
    def _(step):
        @pl.when(step < chunks)
        def _():
            hop(0, step).wait_recv()

            @pl.when(z_sends)
            def _():
                hop(2, step).start()

            @pl.when(outer)
            def _():
                hop(3, step).start()

        @pl.when(jnp.logical_and(step >= 1, step < chunks + 1))
        def _():
            c = step - 1

            @pl.when(z_recvs)
            def _():
                hop(2, c).wait_recv()

                @pl.when(jnp.logical_not(outer))
                def _():
                    hop(3, c).start()

        @pl.when(step >= 2)
        def _():
            c = step - 2
            hop(1, c).wait_recv()

            @pl.when(jnp.logical_or(jnp.logical_not(outer), z_recvs))
            def _():
                hop(3, c).wait_recv()

            @pl.loop(0, pieces)
            def _(piece):
                strip(c * rows + lax.div(piece, lane_blocks) * STRIP, lax.rem(piece, lane_blocks) * LANES)

            store(c).start()

    slot_a = dp * GROUP + r
    n_filt = 8
    for b in range(2):
        f00, f01 = filt[b, 0, 0:1, :], filt[b, 0, 1:2, :]
        f10, f11 = filt[b, 1, 0:1, :], filt[b, 1, 1:2, :]

        def total(k):
            return jnp.sum(sums[b * n_sums + k], axis=0, keepdims=True)

        def put(k, value):
            buf_a[slot_a, k : k + 1, :] = value

        s_y, t_y = total(0), total(1)
        last, w = mix[b, levels : levels + 1, :], mix[b, top : top + 1, :]
        terms = [last * s_y, last * t_y, w * s_y, w * t_y]
        base = n_filt + b * (levels + 1)
        put(base + levels, f00 * s_y + f01 * t_y)
        put(base + top, f10 * s_y + f11 * t_y)
        for level in reversed(range(top)):
            s_a, s_y, t_a, t_y = [total(2 + 4 * level + k) for k in range(4)]
            w = mix[b, level : level + 1, :]
            terms = [u + v for u, v in zip(terms, [s_a, t_a, w * s_y, w * t_y])]
            put(base + level, f10 * s_y + f11 * t_y)
        for k in range(4):
            put(4 * b + k, terms[k])

    def team_copy(a, b):
        to_dp, to_r = team_member(a, b)
        slot = dp * GROUP + r
        return pltpu.make_async_remote_copy(
            src_ref=buf_a.at[slot],
            dst_ref=buf_a.at[slot],
            send_sem=send_a.at[a * GROUP + b],
            recv_sem=recv_a.at[a * GROUP + b],
            device_id=(to_dp, q * GROUP + to_r),
            device_id_type=MESH,
        )

    def group_copy(k):
        to_q = lax.rem(q + k, groups)
        return pltpu.make_async_remote_copy(
            src_ref=buf_b.at[q],
            dst_ref=buf_b.at[q],
            send_sem=send_b.at[k],
            recv_sem=recv_b.at[k],
            device_id=(dp, to_q * GROUP + r),
            device_id_type=MESH,
        )

    for a, b in team:
        team_copy(a, b).start()
    for a, b in team:
        team_copy(a, b).wait_recv()
    value = buf_a[0]
    for k in range(1, n_dp * GROUP):
        value = value + buf_a[k]
    buf_b[q] = value
    for k in range(1, groups):
        group_copy(k).start()
    for k in range(1, groups):
        group_copy(k).wait_recv()
    value = buf_b[0]
    for k in range(1, groups):
        value = value + buf_b[k]
    value = value * factor
    for b in range(2):
        for kind in range(2):
            at = 4 * b + 2 * kind
            out_filt[b, kind] = value[at : at + 2]
        base = n_filt + b * (levels + 1)
        out_mix[b] = value[base : base + levels + 1]

    for a, b in team:
        team_copy(a, b).wait_send()
    for k in range(1, groups):
        group_copy(k).wait_send()

    @pl.loop(0, chunks)
    def _(c):
        hop(0, c).wait_send()
        hop(1, c).wait_send()
        store(c).wait()

        @pl.when(z_sends)
        def _():
            hop(2, c).wait_send()

        @pl.when(jnp.logical_or(outer, z_recvs))
        def _():
            hop(3, c).wait_send()


def body(level_input, saved_forward, saved_reverse, filters, mixing, cotangent):
    n_dp, n_ctx = lax.axis_size("dp"), lax.axis_size("ctx")
    levels = saved_forward.shape[0] + 1
    seqs, span, width = level_input.shape
    units = span // BASE
    assert seqs == 1 and span % BASE == 0 and n_ctx % GROUP == 0
    assert 2**levels <= 2 * units and width % LANES == 0
    rows = STRIP
    chunks = BASE // rows
    top = levels - 1
    groups = n_ctx // GROUP
    factor = 1.0 / math.sqrt(seqs * n_dp * span * n_ctx)
    terms = 8 + 2 * (levels + 1)
    block = (units, BASE, width)
    dma = pltpu.SemaphoreType.DMA
    anywhere = pl.BlockSpec(memory_space=pl.ANY)
    vmem = pl.BlockSpec(memory_space=pltpu.VMEM)
    grad_input, grad_filters, grad_mixing = pl.pallas_call(
        functools.partial(kernel, (n_dp, n_ctx, units, levels, rows, factor)),
        out_shape=(
            jax.ShapeDtypeStruct(block, jnp.bfloat16),
            jax.ShapeDtypeStruct(filters.shape, F32),
            jax.ShapeDtypeStruct(mixing.shape, F32),
        ),
        in_specs=[anywhere] * 4 + [vmem] * 2,
        out_specs=(anywhere, vmem, vmem),
        scratch_shapes=[
            pltpu.VMEM((5,) + block, jnp.bfloat16),
            pltpu.VMEM((2 * levels - 1,) + block, jnp.bfloat16),
            pltpu.VMEM(block, jnp.bfloat16),
            pltpu.VMEM((2 * (2 + 4 * top), STRIP, width), F32),
            pltpu.VMEM((2 * (4 + 2 * top), width), F32),
            pltpu.VMEM((n_dp * GROUP, terms, width), F32),
            pltpu.VMEM((groups, terms, width), F32),
            dma((4,)),
            dma((chunks,)),
            dma((4, chunks)),
            dma((4, chunks)),
            dma((n_dp * GROUP,)),
            dma((n_dp * GROUP,)),
            dma((groups,)),
            dma((groups,)),
        ],
        compiler_params=pltpu.CompilerParams(
            collective_id=0, has_side_effects=True, vmem_limit_bytes=32 * 1024 * 1024
        ),
        cost_estimate=pl.CostEstimate(
            flops=300 * span * width, bytes_accessed=9 * span * width * 2, transcendentals=0
        ),
    )(
        cotangent.reshape(block),
        level_input.reshape(block),
        saved_forward.reshape((top,) + block),
        saved_reverse.reshape((top,) + block),
        filters,
        mixing,
    )
    return (grad_input.reshape(level_input.shape), grad_filters, grad_mixing)


def solution(mesh):
    return jax.shard_map(
        body,
        mesh=mesh,
        in_specs=(
            P("dp", "ctx", None),
            P(None, "dp", "ctx", None),
            P(None, "dp", "ctx", None),
            P(),
            P(),
            P("dp", "ctx", None),
        ),
        out_specs=(P("dp", "ctx", None), P(), P()),
        check_vma=False,
    )
```

time: 190 us -> 45.2 us (0.24)
  the two profiles are of different devices: /device:TPU:1 before, /device:TPU:0 now
where the time goes in v1:
time: 45.2 us; the launch traced here: 44.8 us
  Pallas kernels  35.9 us (79%)
  local copies, waits for them, and re-layouts  8.29 us (18%)
  between operations  0.64 us (1%)
    pallas_call x1, Pallas kernels, body(): pl.pallas_call(functools.partial(kernel, (n_dp, n_ctx, units, levels, row...  35.9 us
    unnamed x14, local copies, waits for them, and re-layouts  8.29 us

profile of v1, /device:TPU:0, one launch (start us, length us, event | category | flops | bytes accessed | tf_op | source)
XLA Modules:
  0.0 44.8 jit_solution(3978411039115087827)
XLA Ops:
  0.6 0.7 %copy.9.mix = f32[2,5,256]{2,1,0:T(8,128)S(1)} copy(f32[2,5,256]{2,0,1:T(2,128)} %param.10) | data formatting | bytes 20480 | tf_op args[4]
  1.3 0.0 copy-start
  1.3 1.4 %copy-done = bf16[3,1,1024,256]{3,2,1,0:T(8,128)(2,1)S(1)} copy-done((bf16[3,1,1024,256]{3,2,1,0:T(8,128)(2,1)S(1)}, bf16[3,1,1024,256]{3,2,1,0:T(8,128)(2,1)}, u32[]{:S(2)}) %copy-start) | copy-done | bytes 1572888
  2.7 0.0 copy-start.1
  2.7 1.4 %copy-done.1 = bf16[3,1,1024,256]{3,2,1,0:T(8,128)(2,1)S(1)} copy-done((bf16[3,1,1024,256]{3,2,1,0:T(8,128)(2,1)S(1)}, bf16[3,1,1024,256]{3,2,1,0:T(8,128)(2,1)}, u32[]{:S(2)}) %copy-start.1) | copy-done | bytes 1572888
  4.2 0.0 copy-start.2
  4.2 1.0 %copy-done.2 = bf16[1,1024,256]{2,1,0:T(8,128)(2,1)S(1)} copy-done((bf16[1,1024,256]{2,1,0:T(8,128)(2,1)S(1)}, bf16[1,1024,256]{2,1,0:T(8,128)(2,1)}, u32[]{:S(2)}) %copy-start.2) | copy-done | bytes 524312
  5.2 0.0 copy-start.3
  5.2 1.0 %copy-done.3 = bf16[1,1024,256]{2,1,0:T(8,128)(2,1)S(1)} copy-done((bf16[1,1024,256]{2,1,0:T(8,128)(2,1)S(1)}, bf16[1,1024,256]{2,1,0:T(8,128)(2,1)}, u32[]{:S(2)}) %copy-start.3) | copy-done | bytes 524312
  6.2 0.0 copy-start.4
  6.2 0.7 %copy-done.4 = f32[2,2,2,256]{3,2,1,0:T(2,128)S(1)} copy-done((f32[2,2,2,256]{3,2,1,0:T(2,128)S(1)}, f32[2,2,2,256]{3,2,1,0:T(2,128)}, u32[]{:S(2)}) %copy-start.4) | copy-done | bytes 8216
  6.9 35.9 %shard_map.85 = (bf16[8,128,256]{2,1,0:T(8,128)(2,1)S(1)}, f32[2,2,2,256]{3,2,1,0:T(2,128)S(1)}, f32[2,5,256]{2,1,0:T(8,128)S(1)}) custom-call(bf16[8,128,256]{2,1,0:T(8,128)(2,1)S(1)} %bitcast.8, bf16[8,128,256]{2,1,0:T(8,128)(2,1)S(1)} %bitcast.9, bf16[3,8,128,256]{3,2,1,0:T(8,128)(2,1)S(1)} %bitcast.5, bf16[3,8,128,256]{3,2,1,0:T(8,128)(2,1)S(1)} %bitcast.6, ...), custom_call_target="tpu_custom_call" | custom-call | flops 78643200 | bytes 4718592 | tf_op jit(solution)/shard_map/pallas_call | solution.py:356
  42.8 0.6 %copy.10 = f32[2,5,256]{2,0,1:T(2,128)} copy(f32[2,5,256]{2,1,0:T(8,128)S(1)} %get-tuple-element.11) | data formatting | bytes 20480
  43.4 0.8 %copy.13 = bf16[1,1024,256]{2,1,0:T(8,128)(2,1)} copy(bf16[1,1024,256]{2,1,0:T(8,128)(2,1)S(1)} %bitcast.7) | data formatting | bytes 1048576
  44.2 0.6 %copy.14 = f32[2,2,2,256]{3,2,1,0:T(2,128)} copy(f32[2,2,2,256]{3,2,1,0:T(2,128)S(1)} %get-tuple-element.16) | data formatting | bytes 16384
Async XLA Ops:
  1.3 1.4 %copy-start = (bf16[3,1,1024,256]{3,2,1,0:T(8,128)(2,1)S(1)}, bf16[3,1,1024,256]{3,2,1,0:T(8,128)(2,1)}, u32[]{:S(2)}) copy-start(bf16[3,1,1024,256]{3,2,1,0:T(8,128)(2,1)} %param.7) | copy-start | bytes 4718596
  2.7 1.4 %copy-start.1 = (bf16[3,1,1024,256]{3,2,1,0:T(8,128)(2,1)S(1)}, bf16[3,1,1024,256]{3,2,1,0:T(8,128)(2,1)}, u32[]{:S(2)}) copy-start(bf16[3,1,1024,256]{3,2,1,0:T(8,128)(2,1)} %param.8) | copy-start | bytes 4718596
  4.2 1.0 %copy-start.2 = (bf16[1,1024,256]{2,1,0:T(8,128)(2,1)S(1)}, bf16[1,1024,256]{2,1,0:T(8,128)(2,1)}, u32[]{:S(2)}) copy-start(bf16[1,1024,256]{2,1,0:T(8,128)(2,1)} %param.11) | copy-start | bytes 1572868
  5.2 1.0 %copy-start.3 = (bf16[1,1024,256]{2,1,0:T(8,128)(2,1)S(1)}, bf16[1,1024,256]{2,1,0:T(8,128)(2,1)}, u32[]{:S(2)}) copy-start(bf16[1,1024,256]{2,1,0:T(8,128)(2,1)} %param.6) | copy-start | bytes 1572868
  6.2 0.7 %copy-start.4 = (f32[2,2,2,256]{3,2,1,0:T(2,128)S(1)}, f32[2,2,2,256]{3,2,1,0:T(2,128)}, u32[]{:S(2)}) copy-start(f32[2,2,2,256]{3,2,1,0:T(2,128)} %filt.1) | copy-start | bytes 24580

commit v2 on v1

--- a/solution.py
+++ b/solution.py
@@ -22,13 +22,15 @@
     first,
     fwd,
     rev,
-    filt,
-    mix,
+    filt_in,
+    mix_in,
     out,
     out_filt,
     out_mix,
     dy,
     inputs,
+    filt,
+    mix,
     result,
     sums,
     coef,
@@ -70,8 +72,11 @@
         pltpu.make_async_copy(fwd, inputs.at[pl.ds(1, top)], load_sem.at[2]),
         pltpu.make_async_copy(rev, inputs.at[pl.ds(levels, top)], load_sem.at[3]),
     ]
-    own_load.start()
-    for load in in_loads:
+    small_loads = [
+        pltpu.make_async_copy(filt_in, filt, load_sem.at[4]),
+        pltpu.make_async_copy(mix_in, mix, load_sem.at[5]),
+    ]
+    for load in small_loads + [own_load] + in_loads:
         load.start()
 
     barrier = pltpu.get_barrier_semaphore()
@@ -122,14 +127,20 @@
     def _():
         dy[1 + 2 * core] = jnp.zeros(dy.shape[1:], dy.dtype)
 
+    for load in small_loads:
+        load.wait()
+
+    def weight(b, level):
+        return mix[level, b : b + 1, :]
+
     per = 4 + 2 * top
     for b in range(2):
         f00, f01 = filt[b, 0, 0:1, :], filt[b, 0, 1:2, :]
         f10, f11 = filt[b, 1, 0:1, :], filt[b, 1, 1:2, :]
-        last, w = mix[b, levels : levels + 1, :], mix[b, top : top + 1, :]
+        last, w = weight(b, levels), weight(b, top)
         values = [f01, f00, f01 * last + f11 * w, f00 * last + f10 * w]
         for level in range(top):
-            w = mix[b, level : level + 1, :]
+            w = weight(b, level)
             values += [f11 * w, f10 * w]
         for k, value in enumerate(values):
             coef[b * per + k : b * per + k + 1, :] = value
@@ -201,9 +212,10 @@
         load.wait()
 
     lane_blocks = width // LANES
+    mid, late = 2, 3
     pieces = (rows // STRIP) * lane_blocks
 
-    @pl.loop(0, chunks + 2)
+    @pl.loop(0, chunks + late)
     def _(step):
         @pl.when(step < chunks)
         def _():
@@ -217,9 +229,9 @@
             def _():
                 hop(3, step).start()
 
-        @pl.when(jnp.logical_and(step >= 1, step < chunks + 1))
+        @pl.when(jnp.logical_and(step >= mid, step < chunks + mid))
         def _():
-            c = step - 1
+            c = step - mid
 
             @pl.when(z_recvs)
             def _():
@@ -229,9 +241,9 @@
                 def _():
                     hop(3, c).start()
 
-        @pl.when(step >= 2)
+        @pl.when(step >= late)
         def _():
-            c = step - 2
+            c = step - late
             hop(1, c).wait_recv()
 
             @pl.when(jnp.logical_or(jnp.logical_not(outer), z_recvs))
@@ -257,14 +269,14 @@
             buf_a[slot_a, k : k + 1, :] = value
 
         s_y, t_y = total(0), total(1)
-        last, w = mix[b, levels : levels + 1, :], mix[b, top : top + 1, :]
+        last, w = weight(b, levels), weight(b, top)
         terms = [last * s_y, last * t_y, w * s_y, w * t_y]
         base = n_filt + b * (levels + 1)
         put(base + levels, f00 * s_y + f01 * t_y)
         put(base + top, f10 * s_y + f11 * t_y)
         for level in reversed(range(top)):
             s_a, s_y, t_a, t_y = [total(2 + 4 * level + k) for k in range(4)]
-            w = mix[b, level : level + 1, :]
+            w = weight(b, level)
             terms = [u + v for u, v in zip(terms, [s_a, t_a, w * s_y, w * t_y])]
             put(base + level, f10 * s_y + f11 * t_y)
         for k in range(4):
@@ -314,7 +326,7 @@
             at = 4 * b + 2 * kind
             out_filt[b, kind] = value[at : at + 2]
         base = n_filt + b * (levels + 1)
-        out_mix[b] = value[base : base + levels + 1]
+        out_mix[:, b] = value[base : base + levels + 1]
 
     for a, b in team:
         team_copy(a, b).wait_send()
@@ -350,27 +362,30 @@
     factor = 1.0 / math.sqrt(seqs * n_dp * span * n_ctx)
     terms = 8 + 2 * (levels + 1)
     block = (units, BASE, width)
+    by_level = mixing.transpose(1, 0, 2)
     dma = pltpu.SemaphoreType.DMA
-    anywhere = pl.BlockSpec(memory_space=pl.ANY)
+    hbm = pl.BlockSpec(memory_space=pltpu.HBM)
     vmem = pl.BlockSpec(memory_space=pltpu.VMEM)
     grad_input, grad_filters, grad_mixing = pl.pallas_call(
         functools.partial(kernel, (n_dp, n_ctx, units, levels, rows, factor)),
         out_shape=(
             jax.ShapeDtypeStruct(block, jnp.bfloat16),
             jax.ShapeDtypeStruct(filters.shape, F32),
-            jax.ShapeDtypeStruct(mixing.shape, F32),
+            jax.ShapeDtypeStruct(by_level.shape, F32),
         ),
-        in_specs=[anywhere] * 4 + [vmem] * 2,
-        out_specs=(anywhere, vmem, vmem),
+        in_specs=[hbm] * 6,
+        out_specs=(hbm, vmem, vmem),
         scratch_shapes=[
             pltpu.VMEM((5,) + block, jnp.bfloat16),
             pltpu.VMEM((2 * levels - 1,) + block, jnp.bfloat16),
+            pltpu.VMEM(filters.shape, F32),
+            pltpu.VMEM(by_level.shape, F32),
             pltpu.VMEM(block, jnp.bfloat16),
             pltpu.VMEM((2 * (2 + 4 * top), STRIP, width), F32),
             pltpu.VMEM((2 * (4 + 2 * top), width), F32),
             pltpu.VMEM((n_dp * GROUP, terms, width), F32),
             pltpu.VMEM((groups, terms, width), F32),
-            dma((4,)),
+            dma((6,)),
             dma((chunks,)),
             dma((4, chunks)),
             dma((4, chunks)),
@@ -380,7 +395,7 @@
             dma((groups,)),
         ],
         compiler_params=pltpu.CompilerParams(
-            collective_id=0, has_side_effects=True, vmem_limit_bytes=32 * 1024 * 1024
+            collective_id=0, has_side_effects=True, vmem_limit_bytes=63 * 1024 * 1024
         ),
         cost_estimate=pl.CostEstimate(
             flops=300 * span * width, bytes_accessed=9 * span * width * 2, transcendentals=0
@@ -391,9 +406,9 @@
         saved_forward.reshape((top,) + block),
         saved_reverse.reshape((top,) + block),
         filters,
-        mixing,
+        by_level,
     )
-    return (grad_input.reshape(level_input.shape), grad_filters, grad_mixing)
+    return (grad_input.reshape(level_input.shape), grad_filters, grad_mixing.transpose(1, 0, 2))
 
 
 def solution(mesh):

time: 45.2 us -> 39.2 us (0.87)
  local copies, waits for them, and re-layouts: 8.29 us -> 4.46 us
  Pallas kernels: 35.9 us -> 33.8 us
    unnamed x14 -> x3, local copies, waits for them, and re-layouts: 8.29 us -> 4.46 us
    pallas_call x1, Pallas kernels: 35.9 us -> 33.8 us  [body(): pl.pallas_call(functools.partial(kernel, (n_dp, n_ctx, units, levels, row...]
where the time goes in v2:
time: 39.2 us; the launch traced here: 38.9 us
  Pallas kernels  33.8 us (86%)
  local copies, waits for them, and re-layouts  4.46 us (11%)
  between operations  0.64 us (2%)
    pallas_call x1, Pallas kernels, body(): pl.pallas_call(functools.partial(kernel, (n_dp, n_ctx, units, levels, row...  33.8 us
    unnamed x3, local copies, waits for them, and re-layouts  4.46 us

profile of v2, /device:TPU:0, one launch (start us, length us, event | category | flops | bytes accessed | tf_op | source)
XLA Modules:
  0.0 38.9 jit_solution(16681773343184941636)
XLA Ops:
  0.6 33.8 %shard_map.85 = (bf16[8,128,256]{2,1,0:T(8,128)(2,1)}, f32[2,2,2,256]{3,2,1,0:T(2,128)}, f32[5,2,256]{2,1,0:T(2,128)}) custom-call(bf16[8,128,256]{2,1,0:T(8,128)(2,1)} %bitcast.10, bf16[8,128,256]{2,1,0:T(8,128)(2,1)} %bitcast.11, bf16[3,8,128,256]{3,2,1,0:T(8,128)(2,1)} %bitcast.7, bf16[3,8,128,256]{3,2,1,0:T(8,128)(2,1)} %bitcast.8, ...), custom_call_target="tpu_custom_call" | custom-call | flops 78643200 | bytes 4718592 | tf_op jit(solution)/shard_map/pallas_call | solution.py:369
  34.5 1.9 %copy.12 = bf16[1,1024,256]{2,1,0:T(8,128)(2,1)} copy(bf16[1,1024,256]{2,1,0:T(8,128)(2,1)} %bitcast.9) | data formatting | bytes 1048576
  36.3 1.3 %copy.13 = f32[2,2,2,256]{3,2,1,0:T(2,128)} copy(f32[2,2,2,256]{3,2,1,0:T(2,128)} %get-tuple-element.13) | data formatting | bytes 16384
  37.6 1.3 %copy.14 = f32[2,5,256]{2,0,1:T(2,128)} copy(f32[2,5,256]{2,0,1:T(2,128)} %bitcast.13) | data formatting | bytes 20480

commit v3 on v2

--- a/solution.py
+++ b/solution.py
@@ -31,13 +31,11 @@
     inputs,
     filt,
     mix,
-    result,
     sums,
     coef,
     buf_a,
     buf_b,
     load_sem,
-    store_sem,
     send_sem,
     recv_sem,
     send_a,
@@ -202,10 +200,7 @@
             for m in range(units):
                 final[place(m)] = g[m] if b == 0 else final[place(m)] + g[m]
         for j in range(units):
-            result[j, rows_at, lanes_at] = final[j].astype(result.dtype)
-
-    def store(c):
-        return pltpu.make_async_copy(part(result, c), part(out, c), store_sem.at[c])
+            out[j, rows_at, lanes_at] = final[j].astype(out.dtype)
 
     own_load.wait()
     for load in in_loads:
@@ -253,8 +248,6 @@
             @pl.loop(0, pieces)
             def _(piece):
                 strip(c * rows + lax.div(piece, lane_blocks) * STRIP, lax.rem(piece, lane_blocks) * LANES)
-
-            store(c).start()
 
     slot_a = dp * GROUP + r
     n_filt = 8
@@ -337,7 +330,6 @@
     def _(c):
         hop(0, c).wait_send()
         hop(1, c).wait_send()
-        store(c).wait()
 
         @pl.when(z_sends)
         def _():
@@ -369,24 +361,22 @@
     grad_input, grad_filters, grad_mixing = pl.pallas_call(
         functools.partial(kernel, (n_dp, n_ctx, units, levels, rows, factor)),
         out_shape=(
-            jax.ShapeDtypeStruct(block, jnp.bfloat16),
-            jax.ShapeDtypeStruct(filters.shape, F32),
-            jax.ShapeDtypeStruct(by_level.shape, F32),
+            pltpu.VMEM(block, jnp.bfloat16),
+            pltpu.VMEM(filters.shape, F32),
+            pltpu.VMEM(by_level.shape, F32),
         ),
         in_specs=[hbm] * 6,
-        out_specs=(hbm, vmem, vmem),
+        out_specs=(vmem, vmem, vmem),
         scratch_shapes=[
             pltpu.VMEM((5,) + block, jnp.bfloat16),
             pltpu.VMEM((2 * levels - 1,) + block, jnp.bfloat16),
             pltpu.VMEM(filters.shape, F32),
             pltpu.VMEM(by_level.shape, F32),
-            pltpu.VMEM(block, jnp.bfloat16),
             pltpu.VMEM((2 * (2 + 4 * top), STRIP, width), F32),
             pltpu.VMEM((2 * (4 + 2 * top), width), F32),
             pltpu.VMEM((n_dp * GROUP, terms, width), F32),
             pltpu.VMEM((groups, terms, width), F32),
             dma((6,)),
-            dma((chunks,)),
             dma((4, chunks)),
             dma((4, chunks)),
             dma((n_dp * GROUP,)),
@@ -395,18 +385,23 @@
             dma((groups,)),
         ],
         compiler_params=pltpu.CompilerParams(
-            collective_id=0, has_side_effects=True, vmem_limit_bytes=63 * 1024 * 1024
+            collective_id=0, has_side_effects=True, vmem_limit_bytes=32 * 1024 * 1024
         ),
         cost_estimate=pl.CostEstimate(
             flops=300 * span * width, bytes_accessed=9 * span * width * 2, transcendentals=0
         ),
     )(
-        cotangent.reshape(block),
-        level_input.reshape(block),
-        saved_forward.reshape((top,) + block),
-        saved_reverse.reshape((top,) + block),
-        filters,
-        by_level,
+        *[
+            pltpu.with_memory_space_constraint(operand, pltpu.HBM)
+            for operand in (
+                cotangent.reshape(block),
+                level_input.reshape(block),
+                saved_forward.reshape((top,) + block),
+                saved_reverse.reshape((top,) + block),
+                filters,
+                by_level,
+            )
+        ]
     )
     return (grad_input.reshape(level_input.shape), grad_filters, grad_mixing.transpose(1, 0, 2))
 

time: 39.2 us -> 35.9 us (0.916)
  local copies, waits for them, and re-layouts: 4.46 us -> 1.99 us
  Pallas kernels: 33.8 us -> 33.1 us
    unnamed x3, local copies, waits for them, and re-layouts: 4.46 us -> 1.99 us
    pallas_call x1, Pallas kernels: 33.8 us -> 33.1 us  [body(): pl.pallas_call(functools.partial(kernel, (n_dp, n_ctx, units, levels, row...]
where the time goes in v3:
time: 35.9 us; the launch traced here: 35.8 us
  Pallas kernels  33.1 us (92%)
  local copies, waits for them, and re-layouts  1.99 us (6%)
  between operations  0.64 us (2%)
    pallas_call x1, Pallas kernels, body(): pl.pallas_call(functools.partial(kernel, (n_dp, n_ctx, units, levels, row...  33.1 us
    unnamed x3, local copies, waits for them, and re-layouts  1.99 us

profile of v3, /device:TPU:0, one launch (start us, length us, event | category | flops | bytes accessed | tf_op | source)
XLA Modules:
  0.0 35.8 jit_solution(12321569265946477311)
XLA Ops:
  0.6 33.1 %shard_map.85 = (bf16[8,128,256]{2,1,0:T(8,128)(2,1)S(1)}, f32[2,2,2,256]{3,2,1,0:T(2,128)S(1)}, f32[5,2,256]{2,1,0:T(2,128)S(1)}) custom-call(bf16[8,128,256]{2,1,0:T(8,128)(2,1)} %bitcast.11, bf16[8,128,256]{2,1,0:T(8,128)(2,1)} %bitcast.12, bf16[3,8,128,256]{3,2,1,0:T(8,128)(2,1)} %bitcast.9, bf16[3,8,128,256]{3,2,1,0:T(8,128)(2,1)} %bitcast.10, ...), custom_call_target="tpu_custom_call" | custom-call | flops 78643200 | bytes 4718592 | tf_op jit(solution)/shard_map/pallas_call | solution.py:361
  33.8 0.8 %copy.12 = bf16[1,1024,256]{2,1,0:T(8,128)(2,1)} copy(bf16[1,1024,256]{2,1,0:T(8,128)(2,1)S(1)} %bitcast.7) | data formatting | bytes 1048576
  34.6 0.6 %copy.13 = f32[2,2,2,256]{3,2,1,0:T(2,128)} copy(f32[2,2,2,256]{3,2,1,0:T(2,128)S(1)} %get-tuple-element.10) | data formatting | bytes 16384
  35.2 0.6 %copy.14 = f32[2,5,256]{2,0,1:T(2,128)} copy(f32[2,5,256]{2,0,1:T(2,128)S(1)} %bitcast.8) | data formatting | bytes 20480

commit v4 on v3

--- a/solution.py
+++ b/solution.py
@@ -31,6 +31,11 @@
     inputs,
     filt,
     mix,
+    dy_wide,
+    inputs_wide,
+    halo,
+    partial,
+    plain_sums,
     sums,
     coef,
     buf_a,
@@ -131,7 +136,6 @@
     def weight(b, level):
         return mix[level, b : b + 1, :]
 
-    per = 4 + 2 * top
     for b in range(2):
         f00, f01 = filt[b, 0, 0:1, :], filt[b, 0, 1:2, :]
         f10, f11 = filt[b, 1, 0:1, :], filt[b, 1, 1:2, :]
@@ -141,74 +145,99 @@
             w = weight(b, level)
             values += [f11 * w, f10 * w]
         for k, value in enumerate(values):
-            coef[b * per + k : b * per + k + 1, :] = value
+            coef[b, k : k + 1, :] = value
     sums[...] = jnp.zeros(sums.shape, F32)
-
-    n_sums = 2 + 4 * top
-
-    def strip(row, lane):
-        rows_at = pl.ds(pl.multiple_of(row, STRIP), STRIP)
-        lanes_at = pl.ds(pl.multiple_of(lane, LANES), LANES)
-        final = [None] * units
-        for b in range(2):
-
-            def place(m):
-                return m % units if b == 0 else units - 1 - m % units
-
-            def dy_at(m):
-                block = 2 + m // units if b == 0 else 2 - m // units
-                return dy[block, place(m), rows_at, lanes_at].astype(F32)
-
-            def input_at(level, m):
-                slot = 0 if level == 0 else (level if b == 0 else level + top)
-                return inputs[slot, place(m), rows_at, lanes_at].astype(F32)
-
-            def factor_at(k):
-                return coef[b * per + k : b * per + k + 1, lanes_at]
-
-            def add(k, value):
-                sums[b * n_sums + k, :, lanes_at] += value
-
-            shift = 2**top
+    plain_sums[...] = jnp.zeros(plain_sums.shape, F32)
+
+    n_sums = 1 + 3 * top
+    lane_blocks = width // LANES
+
+    def window(row, lane):
+        return (
+            pl.ds(pl.multiple_of(row, STRIP), STRIP),
+            pl.ds(pl.multiple_of(lane, LANES), LANES),
+        )
+
+    def pieces(first_row, n_rows, work):
+        @pl.loop(0, (n_rows // STRIP) * lane_blocks)
+        def _(piece):
+            row = first_row + lax.div(piece, lane_blocks) * STRIP
+            work(*window(row, lax.rem(piece, lane_blocks) * LANES))
+
+    def prepare(rows_at, lanes_at):
+        own = []
+        for j in range(units):
+            own.append(dy[2, j, rows_at, lanes_at].astype(F32))
+            dy_wide[j, rows_at, lanes_at] = own[j]
+        for slot in range(2 * levels - 1):
+            t_y = None
+            for j in range(units):
+                p = inputs[slot, j, rows_at, lanes_at].astype(F32)
+                inputs_wide[slot, j, rows_at, lanes_at] = p
+                t_y = own[j] * p if t_y is None else t_y + own[j] * p
+            plain_sums[slot, :, lanes_at] += t_y
+
+    def branch(b, last, rows_at, lanes_at):
+        sign = 1 - 2 * b
+
+        def place(m):
+            return b * (units - 1) + sign * (m % units)
+
+        for m in range(units, units + 2**levels - 1):
+            strip = dy[2 + sign * (m // units), place(m), rows_at, lanes_at]
+            halo[m - units] = strip.astype(F32)
+
+        def dy_at(m):
+            return dy_wide[place(m), rows_at, lanes_at] if m < units else halo[m - units]
+
+        def input_at(level, m):
+            slot = 0 if level == 0 else level + top * b
+            return inputs_wide[slot, place(m), rows_at, lanes_at]
+
+        def factor_at(k):
+            return coef[b, k : k + 1, lanes_at]
+
+        def add(k, value):
+            sums[b * n_sums + k, :, lanes_at] += value
+
+        shift = 2**top
+        y = [dy_at(m) for m in range(units + 2 * shift - 1)]
+        s_y = None
+        for m in range(units):
+            s = y[m + shift] * input_at(top, m)
+            s_y = s if s_y is None else s_y + s
+        add(0, s_y)
+        here, there = factor_at(2), factor_at(3)
+        g = [here * y[m] + there * y[m + shift] for m in range(units + shift - 1)]
+        for level in reversed(range(top)):
+            shift = 2**level
             y = [dy_at(m) for m in range(units + 2 * shift - 1)]
-            s_y = t_y = None
+            acc = None
             for m in range(units):
-                p = input_at(top, m)
-                s, t = y[m + shift] * p, y[m] * p
-                s_y = s if s_y is None else s_y + s
-                t_y = t if t_y is None else t_y + t
-            add(0, s_y)
-            add(1, t_y)
-            here, there = factor_at(2), factor_at(3)
-            g = [here * y[m] + there * y[m + shift] for m in range(units + shift - 1)]
-            for level in reversed(range(top)):
-                shift = 2**level
-                y = [dy_at(m) for m in range(units + 2 * shift - 1)]
-                acc = None
-                for m in range(units):
-                    p = input_at(level, m)
-                    terms = [g[m + shift] * p, y[m + shift] * p, g[m] * p, y[m] * p]
-                    acc = terms if acc is None else [u + v for u, v in zip(acc, terms)]
-                for k in range(4):
-                    add(2 + 4 * level + k, acc[k])
-                f01, f00 = factor_at(0), factor_at(1)
-                w1, w0 = factor_at(4 + 2 * level), factor_at(5 + 2 * level)
-                g = [
-                    f01 * g[m] + w1 * y[m] + (f00 * g[m + shift] + w0 * y[m + shift])
-                    for m in range(units + shift - 1)
-                ]
-            for m in range(units):
-                final[place(m)] = g[m] if b == 0 else final[place(m)] + g[m]
-        for j in range(units):
-            out[j, rows_at, lanes_at] = final[j].astype(out.dtype)
+                p = input_at(level, m)
+                terms = [g[m + shift] * p, y[m + shift] * p, g[m] * p]
+                acc = terms if acc is None else [u + v for u, v in zip(acc, terms)]
+            for k in range(3):
+                add(1 + 3 * level + k, acc[k])
+            f01, f00 = factor_at(0), factor_at(1)
+            w1, w0 = factor_at(4 + 2 * level), factor_at(5 + 2 * level)
+            g = [
+                f01 * g[m] + w1 * y[m] + (f00 * g[m + shift] + w0 * y[m + shift])
+                for m in range(units + shift - 1)
+            ]
+        for m in range(units):
+            if last:
+                total = partial[place(m), rows_at, lanes_at] + g[m]
+                out[place(m), rows_at, lanes_at] = total.astype(out.dtype)
+            else:
+                partial[place(m), rows_at, lanes_at] = g[m]
 
     own_load.wait()
     for load in in_loads:
         load.wait()
-
-    lane_blocks = width // LANES
-    mid, late = 2, 3
-    pieces = (rows // STRIP) * lane_blocks
+    pieces(0, BASE, prepare)
+
+    soon, mid, late = 1, 2, 3
 
     @pl.loop(0, chunks + late)
     def _(step):
@@ -236,18 +265,26 @@
                 def _():
                     hop(3, c).start()
 
-        @pl.when(step >= late)
-        def _():
-            c = step - late
+        @pl.when(jnp.logical_and(step >= soon, step < chunks + soon))
+        def _():
+            c = step - soon
             hop(1, c).wait_recv()
 
-            @pl.when(jnp.logical_or(jnp.logical_not(outer), z_recvs))
+            @pl.when(jnp.logical_not(outer))
             def _():
                 hop(3, c).wait_recv()
 
-            @pl.loop(0, pieces)
-            def _(piece):
-                strip(c * rows + lax.div(piece, lane_blocks) * STRIP, lax.rem(piece, lane_blocks) * LANES)
+            pieces(c * rows, rows, functools.partial(branch, half, False))
+
+        @pl.when(step >= late)
+        def _():
+            c = step - late
+
+            @pl.when(jnp.logical_and(outer, z_recvs))
+            def _():
+                hop(3, c).wait_recv()
+
+            pieces(c * rows, rows, functools.partial(branch, 1 - half, True))
 
     slot_a = dp * GROUP + r
     n_filt = 8
@@ -258,17 +295,22 @@
         def total(k):
             return jnp.sum(sums[b * n_sums + k], axis=0, keepdims=True)
 
+        def plain_total(level):
+            slot = 0 if level == 0 else level + top * b
+            return jnp.sum(plain_sums[slot], axis=0, keepdims=True)
+
         def put(k, value):
             buf_a[slot_a, k : k + 1, :] = value
 
-        s_y, t_y = total(0), total(1)
+        s_y, t_y = total(0), plain_total(top)
         last, w = weight(b, levels), weight(b, top)
         terms = [last * s_y, last * t_y, w * s_y, w * t_y]
         base = n_filt + b * (levels + 1)
         put(base + levels, f00 * s_y + f01 * t_y)
         put(base + top, f10 * s_y + f11 * t_y)
         for level in reversed(range(top)):
-            s_a, s_y, t_a, t_y = [total(2 + 4 * level + k) for k in range(4)]
+            s_a, s_y, t_a = [total(1 + 3 * level + k) for k in range(3)]
+            t_y = plain_total(level)
             w = weight(b, level)
             terms = [u + v for u, v in zip(terms, [s_a, t_a, w * s_y, w * t_y])]
             put(base + level, f10 * s_y + f11 * t_y)
@@ -372,8 +414,13 @@
             pltpu.VMEM((2 * levels - 1,) + block, jnp.bfloat16),
             pltpu.VMEM(filters.shape, F32),
             pltpu.VMEM(by_level.shape, F32),
-            pltpu.VMEM((2 * (2 + 4 * top), STRIP, width), F32),
-            pltpu.VMEM((2 * (4 + 2 * top), width), F32),
+            pltpu.VMEM(block, F32),
+            pltpu.VMEM((2 * levels - 1,) + block, F32),
+            pltpu.VMEM((2**levels - 1, STRIP, LANES), F32),
+            pltpu.VMEM(block, F32),
+            pltpu.VMEM((2 * levels - 1, STRIP, width), F32),
+            pltpu.VMEM((2 * (1 + 3 * top), STRIP, width), F32),
+            pltpu.VMEM((2, 4 + 2 * top, width), F32),
             pltpu.VMEM((n_dp * GROUP, terms, width), F32),
             pltpu.VMEM((groups, terms, width), F32),
             dma((6,)),

time: 35.9 us -> 35.2 us (0.981)
  Pallas kernels: 33.1 us -> 32.4 us
    pallas_call x1, Pallas kernels: 33.1 us -> 32.4 us  [body(): pl.pallas_call(functools.partial(kernel, (n_dp, n_ctx, units, levels, row...]
where the time goes in v4:
time: 35.2 us; the launch traced here: 35.1 us
  Pallas kernels  32.4 us (92%)
  local copies, waits for them, and re-layouts  1.99 us (6%)
  between operations  0.64 us (2%)
    pallas_call x1, Pallas kernels, body(): pl.pallas_call(functools.partial(kernel, (n_dp, n_ctx, units, levels, row...  32.4 us
    unnamed x3, local copies, waits for them, and re-layouts  1.99 us

profile of v4, /device:TPU:0, one launch (start us, length us, event | category | flops | bytes accessed | tf_op | source)
XLA Modules:
  0.0 35.1 jit_solution(3683913638781914489)
XLA Ops:
  0.6 32.4 %shard_map.85 = (bf16[8,128,256]{2,1,0:T(8,128)(2,1)S(1)}, f32[2,2,2,256]{3,2,1,0:T(2,128)S(1)}, f32[5,2,256]{2,1,0:T(2,128)S(1)}) custom-call(bf16[8,128,256]{2,1,0:T(8,128)(2,1)} %bitcast.11, bf16[8,128,256]{2,1,0:T(8,128)(2,1)} %bitcast.12, bf16[3,8,128,256]{3,2,1,0:T(8,128)(2,1)} %bitcast.9, bf16[3,8,128,256]{3,2,1,0:T(8,128)(2,1)} %bitcast.10, ...), custom_call_target="tpu_custom_call" | custom-call | flops 78643200 | bytes 4718592 | tf_op jit(solution)/shard_map/pallas_call | solution.py:403
  33.1 0.8 %copy.12 = bf16[1,1024,256]{2,1,0:T(8,128)(2,1)} copy(bf16[1,1024,256]{2,1,0:T(8,128)(2,1)S(1)} %bitcast.7) | data formatting | bytes 1048576
  33.9 0.6 %copy.13 = f32[2,2,2,256]{3,2,1,0:T(2,128)} copy(f32[2,2,2,256]{3,2,1,0:T(2,128)S(1)} %get-tuple-element.10) | data formatting | bytes 16384
  34.5 0.6 %copy.14 = f32[2,5,256]{2,0,1:T(2,128)} copy(f32[2,5,256]{2,0,1:T(2,128)S(1)} %bitcast.8) | data formatting | bytes 20480

commit v5 on v4

--- a/solution.py
+++ b/solution.py
@@ -12,6 +12,8 @@
 STRIP = 16
 LANES = 128
 GROUP = 4
+HALVES = 2
+AHEAD = 3
 MESH = pl.DeviceIdType.MESH
 F32 = jnp.float32
 
@@ -96,31 +98,36 @@
         pl.semaphore_signal(barrier, inc=1, device_id=(dp, to_q * GROUP + r), device_id_type=MESH)
     pl.semaphore_wait(barrier, len(team) + groups - 1)
 
-    def part(ref, c):
-        return ref.at[:, pl.ds(pl.multiple_of(c * rows, rows), rows), :]
-
-    def hop(kind, c):
+    def part(ref, c, h):
+        some = units // HALVES
+        return ref.at[pl.ds(h * some, some), pl.ds(pl.multiple_of(c * rows, rows), rows), :]
+
+    def hop(kind, c, h):
         if kind == 0:
-            src, slot, to = part(cot, c), 4 * half, partner
+            src, slot, to = cot, 4 * half, partner
         elif kind == 1:
-            src, slot, to = part(cot, c), 1 + 2 * core, sibling
+            src, slot, to = cot, 1 + 2 * core, sibling
         elif kind == 2:
-            src, slot, to = part(dy.at[4 - 4 * half], c), 4 * half, me + 4 - 8 * half
+            src, slot, to = dy.at[4 - 4 * half], 4 * half, me + 4 - 8 * half
         else:
-            src, slot, to = part(dy.at[4 - 4 * core], c), 3 - 2 * core, sibling
+            src, slot, to = dy.at[4 - 4 * core], 3 - 2 * core, sibling
         return pltpu.make_async_remote_copy(
-            src_ref=src,
-            dst_ref=part(dy.at[slot], c),
-            send_sem=send_sem.at[kind, c],
-            recv_sem=recv_sem.at[kind, c],
+            src_ref=part(src, c, h),
+            dst_ref=part(dy.at[slot], c, h),
+            send_sem=send_sem.at[kind, c, h],
+            recv_sem=recv_sem.at[kind, c, h],
             device_id=(dp, to),
             device_id_type=MESH,
         )
 
-    @pl.loop(0, chunks)
-    def _(c):
-        hop(0, c).start()
-        hop(1, c).start()
+    def send_own(c):
+        for kind in range(2):
+            for h in range(HALVES):
+                hop(kind, c, h).start()
+
+    ahead = min(AHEAD, chunks)
+    for c in range(ahead):
+        send_own(c)
 
     @pl.when(jnp.logical_not(z_recvs))
     def _():
@@ -243,15 +250,20 @@
     def _(step):
         @pl.when(step < chunks)
         def _():
-            hop(0, step).wait_recv()
-
-            @pl.when(z_sends)
+            for h in range(HALVES):
+                hop(0, step, h).wait_recv()
+
+                @pl.when(z_sends)
+                def _():
+                    hop(2, step, h).start()
+
+                @pl.when(outer)
+                def _():
+                    hop(3, step, h).start()
+
+            @pl.when(step + ahead < chunks)
             def _():
-                hop(2, step).start()
-
-            @pl.when(outer)
-            def _():
-                hop(3, step).start()
+                send_own(step + ahead)
 
         @pl.when(jnp.logical_and(step >= mid, step < chunks + mid))
         def _():
@@ -259,20 +271,23 @@
 
             @pl.when(z_recvs)
             def _():
-                hop(2, c).wait_recv()
-
-                @pl.when(jnp.logical_not(outer))
-                def _():
-                    hop(3, c).start()
+                for h in range(HALVES):
+                    hop(2, c, h).wait_recv()
+
+                    @pl.when(jnp.logical_not(outer))
+                    def _():
+                        hop(3, c, h).start()
 
         @pl.when(jnp.logical_and(step >= soon, step < chunks + soon))
         def _():
             c = step - soon
-            hop(1, c).wait_recv()
+            for h in range(HALVES):
+                hop(1, c, h).wait_recv()
 
             @pl.when(jnp.logical_not(outer))
             def _():
-                hop(3, c).wait_recv()
+                for h in range(HALVES):
+                    hop(3, c, h).wait_recv()
 
             pieces(c * rows, rows, functools.partial(branch, half, False))
 
@@ -282,7 +297,8 @@
 
             @pl.when(jnp.logical_and(outer, z_recvs))
             def _():
-                hop(3, c).wait_recv()
+                for h in range(HALVES):
+                    hop(3, c, h).wait_recv()
 
             pieces(c * rows, rows, functools.partial(branch, 1 - half, True))
 
@@ -342,6 +358,21 @@
 
     for a, b in team:
         team_copy(a, b).start()
+
+    @pl.loop(0, chunks)
+    def _(c):
+        for h in range(HALVES):
+            hop(0, c, h).wait_send()
+            hop(1, c, h).wait_send()
+
+            @pl.when(z_sends)
+            def _():
+                hop(2, c, h).wait_send()
+
+            @pl.when(jnp.logical_or(outer, z_recvs))
+            def _():
+                hop(3, c, h).wait_send()
+
     for a, b in team:
         team_copy(a, b).wait_recv()
     value = buf_a[0]
@@ -368,18 +399,14 @@
     for k in range(1, groups):
         group_copy(k).wait_send()
 
-    @pl.loop(0, chunks)
-    def _(c):
-        hop(0, c).wait_send()
-        hop(1, c).wait_send()
-
-        @pl.when(z_sends)
-        def _():
-            hop(2, c).wait_send()
-
-        @pl.when(jnp.logical_or(outer, z_recvs))
-        def _():
-            hop(3, c).wait_send()
+
+def hand_over(*refs):
+    sources, targets, sem = refs[:3], refs[3:6], refs[6]
+    copies = [pltpu.make_async_copy(sources[k], targets[k], sem.at[k]) for k in range(3)]
+    for copy in copies:
+        copy.start()
+    for copy in copies:
+        copy.wait()
 
 
 def body(level_input, saved_forward, saved_reverse, filters, mixing, cotangent):
@@ -388,6 +415,7 @@
     seqs, span, width = level_input.shape
     units = span // BASE
     assert seqs == 1 and span % BASE == 0 and n_ctx % GROUP == 0
+    assert units % HALVES == 0
     assert 2**levels <= 2 * units and width % LANES == 0
     rows = STRIP
     chunks = BASE // rows
@@ -424,8 +452,8 @@
             pltpu.VMEM((n_dp * GROUP, terms, width), F32),
             pltpu.VMEM((groups, terms, width), F32),
             dma((6,)),
-            dma((4, chunks)),
-            dma((4, chunks)),
+            dma((4, chunks, HALVES)),
+            dma((4, chunks, HALVES)),
             dma((n_dp * GROUP,)),
             dma((n_dp * GROUP,)),
             dma((groups,)),
@@ -450,6 +478,15 @@
             )
         ]
     )
+    results = (grad_input, grad_filters, grad_mixing)
+    grad_input, grad_filters, grad_mixing = pl.pallas_call(
+        hand_over,
+        out_shape=tuple(pltpu.HBM(x.shape, x.dtype) for x in results),
+        in_specs=[vmem] * 3,
+        out_specs=(hbm,) * 3,
+        scratch_shapes=[dma((3,))],
+        cost_estimate=pl.CostEstimate(flops=0, bytes_accessed=2 * span * width * 2, transcendentals=0),
+    )(*[pltpu.with_memory_space_constraint(x, pltpu.VMEM) for x in results])
     return (grad_input.reshape(level_input.shape), grad_filters, grad_mixing.transpose(1, 0, 2))
 
 

time: 35.2 us -> 34.2 us (0.972)
  local copies, waits for them, and re-layouts: 1.99 us -> 0 us
  Pallas kernels: 32.4 us -> 33.4 us
    unnamed x3 -> x0, local copies, waits for them, and re-layouts: 1.99 us -> none
    pallas_call x0 -> x1, Pallas kernels: none -> 0.83 us  [body(): pl.pallas_call(hand_over, out_shape=tuple((pltpu.HBM(x.shape, x.dtype) fo...]
where the time goes in v5:
time: 34.2 us; the launch traced here: 34.1 us
  Pallas kernels  33.4 us (98%)
  between operations  0.64 us (2%)
    pallas_call x1, Pallas kernels, body(): pl.pallas_call(functools.partial(kernel, (n_dp, n_ctx, units, levels, row...  32.6 us
    pallas_call x1, Pallas kernels, body(): pl.pallas_call(hand_over, out_shape=tuple((pltpu.HBM(x.shape, x.dtype) fo...  0.83 us

profile of v5, /device:TPU:0, one launch (start us, length us, event | category | flops | bytes accessed | tf_op | source)
XLA Modules:
  0.0 34.1 jit_solution(14447916128801192366)
XLA Ops:
  0.6 32.6 %shard_map.85 = (bf16[8,128,256]{2,1,0:T(8,128)(2,1)S(1)}, f32[2,2,2,256]{3,2,1,0:T(2,128)S(1)}, f32[5,2,256]{2,1,0:T(2,128)S(1)}) custom-call(bf16[8,128,256]{2,1,0:T(8,128)(2,1)} %bitcast.9, bf16[8,128,256]{2,1,0:T(8,128)(2,1)} %bitcast.10, bf16[3,8,128,256]{3,2,1,0:T(8,128)(2,1)} %bitcast.7, bf16[3,8,128,256]{3,2,1,0:T(8,128)(2,1)} %bitcast.8, ...), custom_call_target="tpu_custom_call" | custom-call | flops 78643200 | bytes 4718592 | tf_op jit(solution)/shard_map/pallas_call | solution.py:431
  33.2 0.8 %shard_map.86 = (bf16[8,128,256]{2,1,0:T(8,128)(2,1)}, f32[2,2,2,256]{3,2,1,0:T(2,128)}, f32[5,2,256]{2,1,0:T(2,128)}) custom-call(bf16[8,128,256]{2,1,0:T(8,128)(2,1)S(1)} %get-tuple-element.9.refs_0_, f32[2,2,2,256]{3,2,1,0:T(2,128)S(1)} %get-tuple-element.10.refs_1_, f32[5,2,256]{2,1,0:T(2,128)S(1)} %get-tuple-element.11.refs_2_), custom_call_target="tpu_custom_call" | custom-call | bytes 1048576 | tf_op jit(solution)/shard_map/pallas_call | solution.py:482

commit v6 on v5

--- a/solution.py
+++ b/solution.py
@@ -10,6 +10,7 @@
 
 BASE = 128
 STRIP = 16
+TILE = 8
 LANES = 128
 GROUP = 4
 HALVES = 2
@@ -152,26 +153,22 @@
             w = weight(b, level)
             values += [f11 * w, f10 * w]
         for k, value in enumerate(values):
-            coef[b, k : k + 1, :] = value
+            coef[b, k] = jnp.broadcast_to(value, coef.shape[2:])
     sums[...] = jnp.zeros(sums.shape, F32)
     plain_sums[...] = jnp.zeros(plain_sums.shape, F32)
 
     n_sums = 1 + 3 * top
     lane_blocks = width // LANES
 
-    def window(row, lane):
-        return (
-            pl.ds(pl.multiple_of(row, STRIP), STRIP),
-            pl.ds(pl.multiple_of(lane, LANES), LANES),
-        )
-
-    def pieces(first_row, n_rows, work):
-        @pl.loop(0, (n_rows // STRIP) * lane_blocks)
+    def pieces(first_row, n_rows, size, work):
+        @pl.loop(0, (n_rows // size) * lane_blocks)
         def _(piece):
-            row = first_row + lax.div(piece, lane_blocks) * STRIP
-            work(*window(row, lax.rem(piece, lane_blocks) * LANES))
-
-    def prepare(rows_at, lanes_at):
+            row = pl.multiple_of(lax.div(piece, lane_blocks) * size, size)
+            lane = pl.multiple_of(lax.rem(piece, lane_blocks) * LANES, LANES)
+            at = pl.ds(pl.multiple_of(first_row + row, size), size)
+            work(at, pl.ds(row, size), pl.ds(lane, LANES))
+
+    def prepare(rows_at, _, lanes_at):
         own = []
         for j in range(units):
             own.append(dy[2, j, rows_at, lanes_at].astype(F32))
@@ -182,27 +179,28 @@
                 p = inputs[slot, j, rows_at, lanes_at].astype(F32)
                 inputs_wide[slot, j, rows_at, lanes_at] = p
                 t_y = own[j] * p if t_y is None else t_y + own[j] * p
-            plain_sums[slot, :, lanes_at] += t_y
-
-    def branch(b, last, rows_at, lanes_at):
-        sign = 1 - 2 * b
-
-        def place(m):
-            return b * (units - 1) + sign * (m % units)
-
+            plain_sums[slot, :, lanes_at] += t_y[:TILE] + t_y[TILE:]
+
+    def place(b, m):
+        return b * (units - 1) + (1 - 2 * b) * (m % units)
+
+    def widen(b, rows_at, in_chunk, lanes_at):
         for m in range(units, units + 2**levels - 1):
-            strip = dy[2 + sign * (m // units), place(m), rows_at, lanes_at]
-            halo[m - units] = strip.astype(F32)
-
+            strip = dy[2 + (1 - 2 * b) * (m // units), place(b, m), rows_at, lanes_at]
+            halo[m - units, in_chunk, lanes_at] = strip.astype(F32)
+
+    def branch(b, last, rows_at, in_chunk, lanes_at):
         def dy_at(m):
-            return dy_wide[place(m), rows_at, lanes_at] if m < units else halo[m - units]
+            if m < units:
+                return dy_wide[place(b, m), rows_at, lanes_at]
+            return halo[m - units, in_chunk, lanes_at]
 
         def input_at(level, m):
             slot = 0 if level == 0 else level + top * b
-            return inputs_wide[slot, place(m), rows_at, lanes_at]
+            return inputs_wide[slot, place(b, m), rows_at, lanes_at]
 
         def factor_at(k):
-            return coef[b, k : k + 1, lanes_at]
+            return coef[b, k, :, lanes_at]
 
         def add(k, value):
             sums[b * n_sums + k, :, lanes_at] += value
@@ -233,16 +231,17 @@
                 for m in range(units + shift - 1)
             ]
         for m in range(units):
-            if last:
-                total = partial[place(m), rows_at, lanes_at] + g[m]
-                out[place(m), rows_at, lanes_at] = total.astype(out.dtype)
-            else:
-                partial[place(m), rows_at, lanes_at] = g[m]
+            total = partial[place(b, m), rows_at, lanes_at] + g[m] if last else g[m]
+            partial[place(b, m), rows_at, lanes_at] = total
+
+    def finish(rows_at, _, lanes_at):
+        for j in range(units):
+            out[j, rows_at, lanes_at] = partial[j, rows_at, lanes_at].astype(out.dtype)
 
     own_load.wait()
     for load in in_loads:
         load.wait()
-    pieces(0, BASE, prepare)
+    pieces(0, BASE, STRIP, prepare)
 
     soon, mid, late = 1, 2, 3
 
@@ -289,7 +288,8 @@
                 for h in range(HALVES):
                     hop(3, c, h).wait_recv()
 
-            pieces(c * rows, rows, functools.partial(branch, half, False))
+            pieces(c * rows, rows, STRIP, functools.partial(widen, half))
+            pieces(c * rows, rows, TILE, functools.partial(branch, half, False))
 
         @pl.when(step >= late)
         def _():
@@ -300,7 +300,9 @@
                 for h in range(HALVES):
                     hop(3, c, h).wait_recv()
 
-            pieces(c * rows, rows, functools.partial(branch, 1 - half, True))
+            pieces(c * rows, rows, STRIP, functools.partial(widen, 1 - half))
+            pieces(c * rows, rows, TILE, functools.partial(branch, 1 - half, True))
+            pieces(c * rows, rows, STRIP, finish)
 
     slot_a = dp * GROUP + r
     n_filt = 8
@@ -444,11 +446,11 @@
             pltpu.VMEM(by_level.shape, F32),
             pltpu.VMEM(block, F32),
             pltpu.VMEM((2 * levels - 1,) + block, F32),
-            pltpu.VMEM((2**levels - 1, STRIP, LANES), F32),
+            pltpu.VMEM((2**levels - 1, rows, width), F32),
             pltpu.VMEM(block, F32),
-            pltpu.VMEM((2 * levels - 1, STRIP, width), F32),
-            pltpu.VMEM((2 * (1 + 3 * top), STRIP, width), F32),
-            pltpu.VMEM((2, 4 + 2 * top, width), F32),
+            pltpu.VMEM((2 * levels - 1, TILE, width), F32),
+            pltpu.VMEM((2 * (1 + 3 * top), TILE, width), F32),
+            pltpu.VMEM((2, 4 + 2 * top, TILE, width), F32),
             pltpu.VMEM((n_dp * GROUP, terms, width), F32),
             pltpu.VMEM((groups, terms, width), F32),
             dma((6,)),

time: 34.2 us -> 35.2 us (1.029)
  Pallas kernels: 33.4 us -> 34.4 us
    pallas_call x1, Pallas kernels: 32.6 us -> 33.6 us  [body(): pl.pallas_call(functools.partial(kernel, (n_dp, n_ctx, units, levels, row...]
where the time goes in v6:
time: 35.2 us; the launch traced here: 35.1 us
  Pallas kernels  34.4 us (98%)
  between operations  0.64 us (2%)
    pallas_call x1, Pallas kernels, body(): pl.pallas_call(functools.partial(kernel, (n_dp, n_ctx, units, levels, row...  33.6 us
    pallas_call x1, Pallas kernels, body(): pl.pallas_call(hand_over, out_shape=tuple((pltpu.HBM(x.shape, x.dtype) fo...  0.83 us

profile of v6, /device:TPU:0, one launch (start us, length us, event | category | flops | bytes accessed | tf_op | source)
XLA Modules:
  0.0 35.1 jit_solution(2338116885559189080)
XLA Ops:
  0.6 33.6 %shard_map.85 = (bf16[8,128,256]{2,1,0:T(8,128)(2,1)S(1)}, f32[2,2,2,256]{3,2,1,0:T(2,128)S(1)}, f32[5,2,256]{2,1,0:T(2,128)S(1)}) custom-call(bf16[8,128,256]{2,1,0:T(8,128)(2,1)} %bitcast.9, bf16[8,128,256]{2,1,0:T(8,128)(2,1)} %bitcast.10, bf16[3,8,128,256]{3,2,1,0:T(8,128)(2,1)} %bitcast.7, bf16[3,8,128,256]{3,2,1,0:T(8,128)(2,1)} %bitcast.8, ...), custom_call_target="tpu_custom_call" | custom-call | flops 78643200 | bytes 4718592 | tf_op jit(solution)/shard_map/pallas_call | solution.py:433
  34.2 0.8 %shard_map.86 = (bf16[8,128,256]{2,1,0:T(8,128)(2,1)}, f32[2,2,2,256]{3,2,1,0:T(2,128)}, f32[5,2,256]{2,1,0:T(2,128)}) custom-call(bf16[8,128,256]{2,1,0:T(8,128)(2,1)S(1)} %get-tuple-element.9.refs_0_, f32[2,2,2,256]{3,2,1,0:T(2,128)S(1)} %get-tuple-element.10.refs_1_, f32[5,2,256]{2,1,0:T(2,128)S(1)} %get-tuple-element.11.refs_2_), custom_call_target="tpu_custom_call" | custom-call | bytes 1048576 | tf_op jit(solution)/shard_map/pallas_call | solution.py:484

commit v7 on v6

--- a/solution.py
+++ b/solution.py
@@ -36,7 +36,6 @@
     mix,
     dy_wide,
     inputs_wide,
-    halo,
     partial,
     plain_sums,
     sums,
@@ -157,7 +156,6 @@
     sums[...] = jnp.zeros(sums.shape, F32)
     plain_sums[...] = jnp.zeros(plain_sums.shape, F32)
 
-    n_sums = 1 + 3 * top
     lane_blocks = width // LANES
 
     def pieces(first_row, n_rows, size, work):
@@ -168,42 +166,44 @@
             at = pl.ds(pl.multiple_of(first_row + row, size), size)
             work(at, pl.ds(row, size), pl.ds(lane, LANES))
 
+    def place(b, m):
+        return b * (units - 1) + (1 - 2 * b) * (m % units)
+
     def prepare(rows_at, _, lanes_at):
         own = []
         for j in range(units):
             own.append(dy[2, j, rows_at, lanes_at].astype(F32))
-            dy_wide[j, rows_at, lanes_at] = own[j]
+            for b in range(2):
+                dy_wide[b, place(b, j), rows_at, lanes_at] = own[j]
         for slot in range(2 * levels - 1):
+            level = slot if slot < levels else slot - top
             t_y = None
             for j in range(units):
                 p = inputs[slot, j, rows_at, lanes_at].astype(F32)
-                inputs_wide[slot, j, rows_at, lanes_at] = p
+                if slot < levels:
+                    inputs_wide[0, level, j, rows_at, lanes_at] = p
+                if slot == 0 or slot >= levels:
+                    inputs_wide[1, level, place(1, j), rows_at, lanes_at] = p
                 t_y = own[j] * p if t_y is None else t_y + own[j] * p
             plain_sums[slot, :, lanes_at] += t_y[:TILE] + t_y[TILE:]
 
-    def place(b, m):
-        return b * (units - 1) + (1 - 2 * b) * (m % units)
-
-    def widen(b, rows_at, in_chunk, lanes_at):
+    def widen(b, rows_at, _, lanes_at):
         for m in range(units, units + 2**levels - 1):
             strip = dy[2 + (1 - 2 * b) * (m // units), place(b, m), rows_at, lanes_at]
-            halo[m - units, in_chunk, lanes_at] = strip.astype(F32)
-
-    def branch(b, last, rows_at, in_chunk, lanes_at):
+            dy_wide[b, m, rows_at, lanes_at] = strip.astype(F32)
+
+    def branch(b, last, rows_at, _, lanes_at):
         def dy_at(m):
-            if m < units:
-                return dy_wide[place(b, m), rows_at, lanes_at]
-            return halo[m - units, in_chunk, lanes_at]
+            return dy_wide[b, m, rows_at, lanes_at]
 
         def input_at(level, m):
-            slot = 0 if level == 0 else level + top * b
-            return inputs_wide[slot, place(b, m), rows_at, lanes_at]
+            return inputs_wide[b, level, m, rows_at, lanes_at]
 
         def factor_at(k):
             return coef[b, k, :, lanes_at]
 
         def add(k, value):
-            sums[b * n_sums + k, :, lanes_at] += value
+            sums[b, k, :, lanes_at] += value
 
         shift = 2**top
         y = [dy_at(m) for m in range(units + 2 * shift - 1)]
@@ -231,12 +231,14 @@
                 for m in range(units + shift - 1)
             ]
         for m in range(units):
-            total = partial[place(b, m), rows_at, lanes_at] + g[m] if last else g[m]
-            partial[place(b, m), rows_at, lanes_at] = total
+            if last:
+                partial[units - 1 - m, rows_at, lanes_at] += g[m]
+            else:
+                partial[m, rows_at, lanes_at] = g[m]
 
     def finish(rows_at, _, lanes_at):
         for j in range(units):
-            out[j, rows_at, lanes_at] = partial[j, rows_at, lanes_at].astype(out.dtype)
+            out[place(half, j), rows_at, lanes_at] = partial[j, rows_at, lanes_at].astype(out.dtype)
 
     own_load.wait()
     for load in in_loads:
@@ -311,7 +313,7 @@
         f10, f11 = filt[b, 1, 0:1, :], filt[b, 1, 1:2, :]
 
         def total(k):
-            return jnp.sum(sums[b * n_sums + k], axis=0, keepdims=True)
+            return jnp.sum(sums[b, k], axis=0, keepdims=True)
 
         def plain_total(level):
             slot = 0 if level == 0 else level + top * b
@@ -444,12 +446,11 @@
             pltpu.VMEM((2 * levels - 1,) + block, jnp.bfloat16),
             pltpu.VMEM(filters.shape, F32),
             pltpu.VMEM(by_level.shape, F32),
-            pltpu.VMEM(block, F32),
-            pltpu.VMEM((2 * levels - 1,) + block, F32),
-            pltpu.VMEM((2**levels - 1, rows, width), F32),
+            pltpu.VMEM((2, units + 2**levels - 1, BASE, width), F32),
+            pltpu.VMEM((2, levels) + block, F32),
             pltpu.VMEM(block, F32),
             pltpu.VMEM((2 * levels - 1, TILE, width), F32),
-            pltpu.VMEM((2 * (1 + 3 * top), TILE, width), F32),
+            pltpu.VMEM((2, 1 + 3 * top, TILE, width), F32),
             pltpu.VMEM((2, 4 + 2 * top, TILE, width), F32),
             pltpu.VMEM((n_dp * GROUP, terms, width), F32),
             pltpu.VMEM((groups, terms, width), F32),

time: 35.2 us -> 34.8 us (0.989)
  Pallas kernels: 34.4 us -> 34 us
    pallas_call x1, Pallas kernels: 33.6 us -> 33.1 us  [body(): pl.pallas_call(functools.partial(kernel, (n_dp, n_ctx, units, levels, row...]
where the time goes in v7:
time: 34.8 us; the launch traced here: 34.6 us
  Pallas kernels  34 us (98%)
  between operations  0.64 us (2%)
    pallas_call x1, Pallas kernels, body(): pl.pallas_call(functools.partial(kernel, (n_dp, n_ctx, units, levels, row...  33.1 us
    pallas_call x1, Pallas kernels, body(): pl.pallas_call(hand_over, out_shape=tuple((pltpu.HBM(x.shape, x.dtype) fo...  0.83 us

profile of v7, /device:TPU:0, one launch (start us, length us, event | category | flops | bytes accessed | tf_op | source)
XLA Modules:
  0.0 34.6 jit_solution(5585551614727566573)
XLA Ops:
  0.6 33.1 %shard_map.85 = (bf16[8,128,256]{2,1,0:T(8,128)(2,1)S(1)}, f32[2,2,2,256]{3,2,1,0:T(2,128)S(1)}, f32[5,2,256]{2,1,0:T(2,128)S(1)}) custom-call(bf16[8,128,256]{2,1,0:T(8,128)(2,1)} %bitcast.9, bf16[8,128,256]{2,1,0:T(8,128)(2,1)} %bitcast.10, bf16[3,8,128,256]{3,2,1,0:T(8,128)(2,1)} %bitcast.7, bf16[3,8,128,256]{3,2,1,0:T(8,128)(2,1)} %bitcast.8, ...), custom_call_target="tpu_custom_call" | custom-call | flops 78643200 | bytes 4718592 | tf_op jit(solution)/shard_map/pallas_call | solution.py:435
  33.8 0.8 %shard_map.86 = (bf16[8,128,256]{2,1,0:T(8,128)(2,1)}, f32[2,2,2,256]{3,2,1,0:T(2,128)}, f32[5,2,256]{2,1,0:T(2,128)}) custom-call(bf16[8,128,256]{2,1,0:T(8,128)(2,1)S(1)} %get-tuple-element.9.refs_0_, f32[2,2,2,256]{3,2,1,0:T(2,128)S(1)} %get-tuple-element.10.refs_1_, f32[5,2,256]{2,1,0:T(2,128)S(1)} %get-tuple-element.11.refs_2_), custom_call_target="tpu_custom_call" | custom-call | bytes 1048576 | tf_op jit(solution)/shard_map/pallas_call | solution.py:485

commit v8 on v7

--- a/solution.py
+++ b/solution.py
@@ -14,7 +14,7 @@
 LANES = 128
 GROUP = 4
 HALVES = 2
-AHEAD = 3
+AHEAD = 2
 MESH = pl.DeviceIdType.MESH
 F32 = jnp.float32
 
@@ -200,10 +200,10 @@
             return inputs_wide[b, level, m, rows_at, lanes_at]
 
         def factor_at(k):
-            return coef[b, k, :, lanes_at]
+            return coef[b, k, 0:1, lanes_at]
 
         def add(k, value):
-            sums[b, k, :, lanes_at] += value
+            sums[b, k, :, lanes_at] += value[:TILE] + value[TILE:]
 
         shift = 2**top
         y = [dy_at(m) for m in range(units + 2 * shift - 1)]
@@ -245,7 +245,7 @@
         load.wait()
     pieces(0, BASE, STRIP, prepare)
 
-    soon, mid, late = 1, 2, 3
+    soon, mid, late = 1, 1, 2
 
     @pl.loop(0, chunks + late)
     def _(step):
@@ -291,7 +291,7 @@
                     hop(3, c, h).wait_recv()
 
             pieces(c * rows, rows, STRIP, functools.partial(widen, half))
-            pieces(c * rows, rows, TILE, functools.partial(branch, half, False))
+            pieces(c * rows, rows, STRIP, functools.partial(branch, half, False))
 
         @pl.when(step >= late)
         def _():
@@ -303,7 +303,7 @@
                     hop(3, c, h).wait_recv()
 
             pieces(c * rows, rows, STRIP, functools.partial(widen, 1 - half))
-            pieces(c * rows, rows, TILE, functools.partial(branch, 1 - half, True))
+            pieces(c * rows, rows, STRIP, functools.partial(branch, 1 - half, True))
             pieces(c * rows, rows, STRIP, finish)
 
     slot_a = dp * GROUP + r
@@ -421,7 +421,7 @@
     assert seqs == 1 and span % BASE == 0 and n_ctx % GROUP == 0
     assert units % HALVES == 0
     assert 2**levels <= 2 * units and width % LANES == 0
-    rows = STRIP
+    rows = 2 * STRIP
     chunks = BASE // rows
     top = levels - 1
     groups = n_ctx // GROUP

time: 34.8 us -> 35.4 us (1.017)
  Pallas kernels: 34 us -> 34.6 us
    pallas_call x1, Pallas kernels: 33.1 us -> 33.8 us  [body(): pl.pallas_call(functools.partial(kernel, (n_dp, n_ctx, units, levels, row...]
where the time goes in v8:
time: 35.4 us; the launch traced here: 35.3 us
  Pallas kernels  34.6 us (98%)
  between operations  0.64 us (2%)
    pallas_call x1, Pallas kernels, body(): pl.pallas_call(functools.partial(kernel, (n_dp, n_ctx, units, levels, row...  33.8 us
    pallas_call x1, Pallas kernels, body(): pl.pallas_call(hand_over, out_shape=tuple((pltpu.HBM(x.shape, x.dtype) fo...  0.83 us

profile of v8, /device:TPU:0, one launch (start us, length us, event | category | flops | bytes accessed | tf_op | source)
XLA Modules:
  0.0 35.3 jit_solution(11267324756875127919)
XLA Ops:
  0.6 33.8 %shard_map.85 = (bf16[8,128,256]{2,1,0:T(8,128)(2,1)S(1)}, f32[2,2,2,256]{3,2,1,0:T(2,128)S(1)}, f32[5,2,256]{2,1,0:T(2,128)S(1)}) custom-call(bf16[8,128,256]{2,1,0:T(8,128)(2,1)} %bitcast.9, bf16[8,128,256]{2,1,0:T(8,128)(2,1)} %bitcast.10, bf16[3,8,128,256]{3,2,1,0:T(8,128)(2,1)} %bitcast.7, bf16[3,8,128,256]{3,2,1,0:T(8,128)(2,1)} %bitcast.8, ...), custom_call_target="tpu_custom_call" | custom-call | flops 78643200 | bytes 4718592 | tf_op jit(solution)/shard_map/pallas_call | solution.py:435
  34.4 0.8 %shard_map.86 = (bf16[8,128,256]{2,1,0:T(8,128)(2,1)}, f32[2,2,2,256]{3,2,1,0:T(2,128)}, f32[5,2,256]{2,1,0:T(2,128)}) custom-call(bf16[8,128,256]{2,1,0:T(8,128)(2,1)S(1)} %get-tuple-element.9.refs_0_, f32[2,2,2,256]{3,2,1,0:T(2,128)S(1)} %get-tuple-element.10.refs_1_, f32[5,2,256]{2,1,0:T(2,128)S(1)} %get-tuple-element.11.refs_2_), custom_call_target="tpu_custom_call" | custom-call | bytes 1048576 | tf_op jit(solution)/shard_map/pallas_call | solution.py:485

commit v9 on v8

--- a/solution.py
+++ b/solution.py
@@ -14,7 +14,7 @@
 LANES = 128
 GROUP = 4
 HALVES = 2
-AHEAD = 2
+AHEAD = 4
 MESH = pl.DeviceIdType.MESH
 F32 = jnp.float32
 
@@ -243,15 +243,16 @@
     own_load.wait()
     for load in in_loads:
         load.wait()
-    pieces(0, BASE, STRIP, prepare)
-
-    soon, mid, late = 1, 1, 2
+    early = chunks // 2
+    pieces(0, early * rows, STRIP, prepare)
+
+    soon, mid, late = 1, 2, 3
 
     @pl.loop(0, chunks + late)
     def _(step):
-        @pl.when(step < chunks)
-        def _():
-            for h in range(HALVES):
+        def forward(h):
+            @pl.when(step < chunks)
+            def _():
                 hop(0, step, h).wait_recv()
 
                 @pl.when(z_sends)
@@ -262,22 +263,7 @@
                 def _():
                     hop(3, step, h).start()
 
-            @pl.when(step + ahead < chunks)
-            def _():
-                send_own(step + ahead)
-
-        @pl.when(jnp.logical_and(step >= mid, step < chunks + mid))
-        def _():
-            c = step - mid
-
-            @pl.when(z_recvs)
-            def _():
-                for h in range(HALVES):
-                    hop(2, c, h).wait_recv()
-
-                    @pl.when(jnp.logical_not(outer))
-                    def _():
-                        hop(3, c, h).start()
+        forward(0)
 
         @pl.when(jnp.logical_and(step >= soon, step < chunks + soon))
         def _():
@@ -292,6 +278,30 @@
 
             pieces(c * rows, rows, STRIP, functools.partial(widen, half))
             pieces(c * rows, rows, STRIP, functools.partial(branch, half, False))
+
+        for h in range(1, HALVES):
+            forward(h)
+
+        @pl.when(step + ahead < chunks)
+        def _():
+            send_own(step + ahead)
+
+        @pl.when(step + early < chunks)
+        def _():
+            pieces((step + early) * rows, rows, STRIP, prepare)
+
+        @pl.when(jnp.logical_and(step >= mid, step < chunks + mid))
+        def _():
+            c = step - mid
+
+            @pl.when(z_recvs)
+            def _():
+                for h in range(HALVES):
+                    hop(2, c, h).wait_recv()
+
+                    @pl.when(jnp.logical_not(outer))
+                    def _():
+                        hop(3, c, h).start()
 
         @pl.when(step >= late)
         def _():
@@ -421,7 +431,7 @@
     assert seqs == 1 and span % BASE == 0 and n_ctx % GROUP == 0
     assert units % HALVES == 0
     assert 2**levels <= 2 * units and width % LANES == 0
-    rows = 2 * STRIP
+    rows = STRIP
     chunks = BASE // rows
     top = levels - 1
     groups = n_ctx // GROUP

time: 35.4 us -> 33.9 us (0.958)
  Pallas kernels: 34.6 us -> 33.1 us
    pallas_call x1, Pallas kernels: 33.8 us -> 32.3 us  [body(): pl.pallas_call(functools.partial(kernel, (n_dp, n_ctx, units, levels, row...]
where the time goes in v9:
time: 33.9 us; the launch traced here: 33.8 us
  Pallas kernels  33.1 us (98%)
  between operations  0.64 us (2%)
    pallas_call x1, Pallas kernels, body(): pl.pallas_call(functools.partial(kernel, (n_dp, n_ctx, units, levels, row...  32.3 us
    pallas_call x1, Pallas kernels, body(): pl.pallas_call(hand_over, out_shape=tuple((pltpu.HBM(x.shape, x.dtype) fo...  0.83 us

profile of v9, /device:TPU:0, one launch (start us, length us, event | category | flops | bytes accessed | tf_op | source)
XLA Modules:
  0.0 33.8 jit_solution(4847125421849099525)
XLA Ops:
  0.6 32.3 %shard_map.85 = (bf16[8,128,256]{2,1,0:T(8,128)(2,1)S(1)}, f32[2,2,2,256]{3,2,1,0:T(2,128)S(1)}, f32[5,2,256]{2,1,0:T(2,128)S(1)}) custom-call(bf16[8,128,256]{2,1,0:T(8,128)(2,1)} %bitcast.9, bf16[8,128,256]{2,1,0:T(8,128)(2,1)} %bitcast.10, bf16[3,8,128,256]{3,2,1,0:T(8,128)(2,1)} %bitcast.7, bf16[3,8,128,256]{3,2,1,0:T(8,128)(2,1)} %bitcast.8, ...), custom_call_target="tpu_custom_call" | custom-call | flops 78643200 | bytes 4718592 | tf_op jit(solution)/shard_map/pallas_call | solution.py:445
  32.9 0.8 %shard_map.86 = (bf16[8,128,256]{2,1,0:T(8,128)(2,1)}, f32[2,2,2,256]{3,2,1,0:T(2,128)}, f32[5,2,256]{2,1,0:T(2,128)}) custom-call(bf16[8,128,256]{2,1,0:T(8,128)(2,1)S(1)} %get-tuple-element.9.refs_0_, f32[2,2,2,256]{3,2,1,0:T(2,128)S(1)} %get-tuple-element.10.refs_1_, f32[5,2,256]{2,1,0:T(2,128)S(1)} %get-tuple-element.11.refs_2_), custom_call_target="tpu_custom_call" | custom-call | bytes 1048576 | tf_op jit(solution)/shard_map/pallas_call | solution.py:495
